TPU v7x, 128 devices: a whole 4x4x4 slice. The times are simulated.
128 devices in a mesh: dp: 16 (over x_lo, y, core), tensor: 8 (over z, x_hi).
Axes of the slice: x: 4 (x_hi: 2, x_lo: 2; x = x_hi * 2 + x_lo), y: 4, z: 4, core: 2. Of those that a mesh axis runs over, the one named last changes fastest.
Arguments:
- tokens: bfloat16 [4096, 6144], P('dp', 'tensor'), may hold values from -6 to 6
- blocks: bfloat16 [4, 6144, 3072], P(None, 'tensor'), may hold values from -0.109375 to 0.109375
- left_factor: bfloat16 [6144, 256], P('tensor'), may hold values from -0.078125 to 0.078125
- right_factor: bfloat16 [256, 24576], P(None, 'tensor'), may hold values from -0.375 to 0.375
- upstream: bfloat16 [4096, 24576], P('dp', 'tensor'), may hold values from -6 to 6
Outputs:
- activated: bfloat16 [4096, 24576], P('dp', 'tensor')
- token_grad: bfloat16 [4096, 6144], P('dp', 'tensor')
- left_grad: bfloat16 [6144, 256], P('tensor')
- right_grad: bfloat16 [256, 24576], P(None, 'tensor')
All inputs are finite; a program needn't handle non-finite values.
Results may differ from a plain program's by a relative error of at most 0.0063.
Values may be sent and summed in bfloat16 or wider, within the bound.
A program may use at most 128 MiB of HBM per device.

v0:
```python
import jax
import jax.numpy as jnp
from jax import lax
from jax.sharding import PartitionSpec as P


def partner_2(block, axis, distance):
    count = lax.axis_size(axis)
    route = []
    for low in range(count):
        high = low | 1 << distance
        if high != low and high < count:
            route += [(low, high), (high, low)]
    return lax.ppermute(block, axis, route)


def across(left, right, left_dim, right_dim):
    return lax.dot_general(
        left, right, (((left_dim,), (right_dim,)), ((), ())), preferred_element_type=jnp.float32
    )


def body(tokens, blocks, left_factor, right_factor, upstream):
    levels = blocks.shape[0] - 1
    row_count = tokens.shape[0]
    low_part = jnp.dot(tokens, left_factor, preferred_element_type=jnp.float32)
    low_rank = lax.psum(low_part, "tensor").astype(jnp.bfloat16)
    preact = jnp.dot(tokens, blocks[0], preferred_element_type=jnp.float32)
    preact = preact + jnp.dot(low_rank, right_factor, preferred_element_type=jnp.float32)
    for bit_index in range(levels):
        partner = partner_2(tokens, "tensor", bit_index)
        preact = preact + jnp.dot(
            partner, blocks[bit_index + 1], preferred_element_type=jnp.float32
        )
    gelu_out, pullback = jax.vjp(jax.nn.gelu, preact)
    activated = gelu_out.astype(jnp.bfloat16)
    slopes = pullback(upstream.astype(jnp.float32))[0].astype(jnp.bfloat16)
    mixed_part = across(slopes, right_factor, 1, 1)
    mixed_rows = lax.psum(mixed_part, "tensor").astype(jnp.bfloat16)
    norm_scale = 1.0 / jnp.sqrt(jnp.float32(row_count * lax.axis_size("dp")))
    left_part = across(tokens, mixed_rows, 0, 0) * norm_scale
    running = across(slopes, blocks[0], 1, 1) + across(mixed_rows, left_factor, 1, 1)
    for bit_index in range(levels):
        partial_value = across(slopes, blocks[bit_index + 1], 1, 1)
        running = running + partner_2(partial_value, "tensor", bit_index)
    token_grad = running.astype(jnp.bfloat16)
    right_part = across(low_rank, slopes, 0, 0) * norm_scale
    left_total, right_total = lax.psum((left_part, right_part), "dp")
    return (
        activated,
        token_grad,
        left_total.astype(jnp.bfloat16),
        right_total.astype(jnp.bfloat16),
    )


def solution(mesh):
    placed = (
        P("dp", "tensor"),
        P(None, "tensor", None),
        P("tensor", None),
        P(None, "tensor"),
        P("dp", "tensor"),
    )
    return jax.shard_map(
        body,
        mesh=mesh,
        in_specs=placed,
        out_specs=(P("dp", "tensor"), P("dp", "tensor"), P("tensor", None), P(None, "tensor")),
        check_vma=False,
    )
```

profile of v0, /device:TPU:1, one launch (start us, length us, event | category | flops | bytes accessed | tf_op | source)
XLA Modules:
  0.0 213.8 jit_solution(10389991800530434926)
XLA Ops:
  0.6 0.0 copy-start
  0.6 2.5 %collective-permute-start.1 = (bf16[256,768]{1,0:T(8,128)(2,1)}, bf16[256,768]{1,0:T(8,128)(2,1)S(1)}, u32[]{:S(2)}, u32[]{:S(2)}) collective-permute-start(bf16[256,768]{1,0:T(8,128)(2,1)} %param.5), channel_id=1, source_target_pairs={{0,2},{2,0},{1,3},{3,1},{4,6},{6,4},{5,7},{7,5},{8,10},{10,8},{9,1... | collective-permute-start | bytes 1179656 | tf_op jit(solution)/shard_map/ppermute | solution.py:14
  3.2 2.7 %collective-permute-start = (bf16[256,768]{1,0:T(8,128)(2,1)}, bf16[256,768]{1,0:T(8,128)(2,1)S(1)}, u32[]{:S(2)}, u32[]{:S(2)}) collective-permute-start(bf16[256,768]{1,0:T(8,128)(2,1)} %param.5), channel_id=1, source_target_pairs={{0,1},{1,0},{2,3},{3,2},{4,5},{5,4},{6,7},{7,6},{8,9},{9,8},{10,11... | collective-permute-start | bytes 1179656 | tf_op jit(solution)/shard_map/ppermute | solution.py:14
  5.9 3.3 %collective-permute-start.2 = (bf16[256,768]{1,0:T(8,128)(2,1)}, bf16[256,768]{1,0:T(8,128)(2,1)S(1)}, u32[]{:S(2)}, u32[]{:S(2)}) collective-permute-start(bf16[256,768]{1,0:T(8,128)(2,1)} %param.5), channel_id=1, source_target_pairs={{0,4},{4,0},{1,5},{5,1},{2,6},{6,2},{3,7},{7,3},{8,12},{12,8},{9,1... | collective-permute-start | bytes 1179656 | tf_op jit(solution)/shard_map/ppermute | solution.py:14
  9.2 1.4 fusion.52
  10.6 37.5 %all-reduce.4 = bf16[256,256]{1,0:T(8,128)(2,1)S(1)} all-reduce(f32[256,256]{1,0:T(8,128)S(1)} %fusion.52), channel_id=1, replica_groups=mesh['dp'=16,'tensor'=8] {'tensor'}, use_global_device_ids=true, to_apply=%region_0.0 | all-reduce | flops 65536 | bytes 393216 | tf_op jit(solution)/shard_map/psum | solution.py:27
  48.1 0.0 copy-start.3
  48.1 0.0 copy-start.6
  48.1 4.0 %fusion.14 = f32[256,3072]{1,0:T(8,128)S(1)} fusion(bf16[256,768]{1,0:T(8,128)(2,1)} %param.5, bf16[4,768,3072]{2,1,0:T(8,128)(2,1)} %param.6), kind=kOutput, calls=%fused_computation.14 | convolution fusion | flops 1207959552 | bytes 8257536 | tf_op jit(solution)/shard_map/dot_general | solution.py:28
  52.1 0.0 copy-done.3
  52.1 0.0 copy-done
  52.1 0.6 convolution_add_fusion
  52.8 0.0 collective-permute-done.2
  52.8 6.1 %fusion.2 = f32[256,3072]{1,0:T(8,128)} fusion(bf16[256,768]{1,0:T(8,128)(2,1)S(1)} %collective-permute-done.2, bf16[4,768,3072]{2,1,0:T(8,128)(2,1)} %param.6), kind=kOutput, calls=%fused_computation.2 | convolution fusion | flops 1207959552 | bytes 8257536 | tf_op jit(solution)/shard_map/dot_general | solution.py:32
  58.9 0.0 copy-start.7
  58.9 0.0 collective-permute-done.1
  58.9 0.0 copy-done.6
  58.9 3.1 %fusion.6 = f32[256,3072]{1,0:T(8,128)} fusion(bf16[256,768]{1,0:T(8,128)(2,1)S(1)} %collective-permute-done.1, bf16[4,768,3072]{2,1,0:T(8,128)(2,1)S(1)} %copy-done.6), kind=kOutput, calls=%fused_computation.6 | convolution fusion | flops 1207959552 | bytes 8257536 | tf_op jit(solution)/shard_map/dot_general | solution.py:32
  62.0 0.0 collective-permute-done
  62.0 0.0 copy-done.7
  62.0 6.9 %fusion.35 = (bf16[256,3072]{1,0:T(8,128)(2,1)S(1)}, bf16[256,3072]{1,0:T(8,128)(2,1)}) fusion(bf16[256,3072]{1,0:T(8,128)(2,1)S(1)} %copy-done.7, f32[256,3072]{1,0:T(8,128)} %fusion.2, f32[256,3072]{1,0:T(8,128)} %fusion.6, f32[256,3072]{1,0:T(8,128)S(1)} %convolution_add_fusion, bf16[256,768]{1,0:T(8,128)(2,1)S(1)} %collective-permute-done, ...), kind=kOutput, calls=%fused_computation.35 | convolution fusion | flops 1228406784 | bytes 19267584 | tf_op jit(solution)/shard_map/dot_general | solution.py:32
  68.9 1.3 fusion.53
  70.2 2.4 %fusion = f32[256,768]{1,0:T(8,128)} fusion(bf16[256,3072]{1,0:T(8,128)(2,1)S(1)} %get-tuple-element.10, bf16[4,768,3072]{2,1,0:T(8,128)(2,1)S(1)} %copy-done.6), kind=kOutput, calls=%fused_computation | convolution fusion | flops 1207959552 | bytes 7077888 | tf_op jit(solution)/shard_map/dot_general | solution.py:18
  72.7 2.4 %fusion.4 = f32[256,768]{1,0:T(8,128)} fusion(bf16[256,3072]{1,0:T(8,128)(2,1)S(1)} %get-tuple-element.10, bf16[4,768,3072]{2,1,0:T(8,128)(2,1)S(1)} %copy-done.6), kind=kOutput, calls=%fused_computation.4 | convolution fusion | flops 1207959552 | bytes 7077888 | tf_op jit(solution)/shard_map/dot_general | solution.py:18
  75.1 0.0 copy-start.4
  75.1 2.4 %fusion.8 = f32[256,768]{1,0:T(8,128)} fusion(bf16[256,3072]{1,0:T(8,128)(2,1)S(1)} %get-tuple-element.10, bf16[4,768,3072]{2,1,0:T(8,128)(2,1)S(1)} %copy-done.6), kind=kOutput, calls=%fused_computation.8 | convolution fusion | flops 1207959552 | bytes 7077888 | tf_op jit(solution)/shard_map/dot_general | solution.py:18
  77.6 0.0 copy-done.4
  77.6 0.0 copy-start.1
  77.6 2.2 %convolution_multiply_fusion = f32[256,3072]{1,0:T(8,128)} fusion(bf16[256,3072]{1,0:T(8,128)(2,1)S(1)} %get-tuple-element.10, bf16[256,256]{1,0:T(8,128)(2,1)S(1)} %copy-done.4), kind=kOutput, calls=%fused_computation.26 | convolution fusion | flops 403439616 | bytes 4849664 | tf_op jit(solution)/shard_map/dot_general | solution.py:18
  79.8 35.5 %all-reduce.5 = bf16[256,256]{1,0:T(8,128)(2,1)} all-reduce(f32[256,256]{1,0:T(8,128)} %fusion.53), channel_id=1, replica_groups=mesh['dp'=16,'tensor'=8] {'tensor'}, use_global_device_ids=true, to_apply=%region_1.0 | all-reduce | flops 65536 | bytes 393216 | tf_op jit(solution)/shard_map/psum | solution.py:39
  115.3 0.0 copy-done.1
  115.3 2.2 %fusion.43 = f32[768,256]{0,1:T(8,128)} fusion(bf16[256,768]{1,0:T(8,128)(2,1)S(1)} %copy-done.1, bf16[256,256]{1,0:T(8,128)(2,1)} %all-reduce.5), kind=kOutput, calls=%fused_computation.45 | convolution fusion | flops 100859904 | bytes 1310720 | tf_op jit(solution)/shard_map/dot_general | solution.py:18
  117.5 0.9 collective-permute-start.3
  118.4 0.0 collective-permute-start.4
  118.4 3.9 %collective-permute-start.5 = (f32[256,768]{1,0:T(8,128)}, f32[256,768]{1,0:T(8,128)}, u32[]{:S(2)}, u32[]{:S(2)}) collective-permute-start(f32[256,768]{1,0:T(8,128)} %fusion), channel_id=1, source_target_pairs={{0,4},{4,0},{1,5},{5,1},{2,6},{6,2},{3,7},{7,3},{8,12},{12,8},{9,1... | collective-permute-start | bytes 2359304 | tf_op jit(solution)/shard_map/ppermute | solution.py:14
  122.4 84.0 %all-reduce.6 = (bf16[768,256]{0,1:T(8,128)(2,1)S(1)}, bf16[256,3072]{1,0:T(8,128)(2,1)}) all-reduce(f32[768,256]{0,1:T(8,128)} %fusion.43, f32[256,3072]{1,0:T(8,128)} %convolution_multiply_fusion), channel_id=1, replica_groups=mesh['dp'=16,'tensor'=8] {'dp'}, use_global_device_ids=true, to_apply=%region_2.0 | all-reduce | flops 983040 | bytes 5898240 | tf_op jit(solution)/shard_map/psum | solution.py:48
  206.3 0.9 copy.9
  207.2 0.0 copy-start.2
  207.2 0.0 copy-start.5
  207.2 3.8 %fusion.12 = f32[256,768]{1,0:T(8,128)S(1)} fusion(bf16[256,3072]{1,0:T(8,128)(2,1)S(1)} %get-tuple-element.10, bf16[4,768,3072]{2,1,0:T(8,128)(2,1)} %param.6), kind=kOutput, calls=%fused_computation.12 | convolution fusion | flops 1207959552 | bytes 7077888 | tf_op jit(solution)/shard_map/dot_general | solution.py:18
  211.1 0.0 collective-permute-done.3
  211.1 0.0 collective-permute-done.4
  211.1 0.0 collective-permute-done.5
  211.1 0.0 copy-done.2
  211.1 0.0 copy-done.5
  211.1 2.7 %fusion.47 = bf16[256,768]{1,0:T(8,128)(2,1)} fusion(f32[256,768]{1,0:T(8,128)} %collective-permute-done.5, f32[256,768]{1,0:T(8,128)} %collective-permute-done.4, f32[256,768]{1,0:T(8,128)} %collective-permute-done.3, f32[256,768]{1,0:T(8,128)S(1)} %fusion.12, bf16[768,256]{1,0:T(8,128)(2,1)S(1)} %copy-done.2, bf16[256,256]{1,0:T(8,128)(2,1)S(1)} %copy-done.5), kind=kOutput, calls=%fused_computation.50 | convolution fusion | flops 101646336 | bytes 4063232 | tf_op jit(solution)/shard_map/dot_general | solution.py:18
Async XLA Ops:
  0.6 51.5 %copy-start = (bf16[256,3072]{1,0:T(8,128)(2,1)S(1)}, bf16[256,3072]{1,0:T(8,128)(2,1)}, u32[]{:S(2)}) copy-start(bf16[256,3072]{1,0:T(8,128)(2,1)} %param.8) | copy-start | bytes 4718596
  0.6 58.3 %collective-permute-start.1 = (bf16[256,768]{1,0:T(8,128)(2,1)}, bf16[256,768]{1,0:T(8,128)(2,1)S(1)}, u32[]{:S(2)}, u32[]{:S(2)}) collective-permute-start(bf16[256,768]{1,0:T(8,128)(2,1)} %param.5), channel_id=1, source_target_pairs={{0,2},{2,0},{1,3},{3,1},{4,6},{6,4},{5,7},{7,5},{8,10},{10,8},{9,1... | collective-permute-start | bytes 1179656 | tf_op jit(solution)/shard_map/ppermute | solution.py:14
  3.2 58.8 %collective-permute-start = (bf16[256,768]{1,0:T(8,128)(2,1)}, bf16[256,768]{1,0:T(8,128)(2,1)S(1)}, u32[]{:S(2)}, u32[]{:S(2)}) collective-permute-start(bf16[256,768]{1,0:T(8,128)(2,1)} %param.5), channel_id=1, source_target_pairs={{0,1},{1,0},{2,3},{3,2},{4,5},{5,4},{6,7},{7,6},{8,9},{9,8},{10,11... | collective-permute-start | bytes 1179656 | tf_op jit(solution)/shard_map/ppermute | solution.py:14
  5.9 46.8 %collective-permute-start.2 = (bf16[256,768]{1,0:T(8,128)(2,1)}, bf16[256,768]{1,0:T(8,128)(2,1)S(1)}, u32[]{:S(2)}, u32[]{:S(2)}) collective-permute-start(bf16[256,768]{1,0:T(8,128)(2,1)} %param.5), channel_id=1, source_target_pairs={{0,4},{4,0},{1,5},{5,1},{2,6},{6,2},{3,7},{7,3},{8,12},{12,8},{9,1... | collective-permute-start | bytes 1179656 | tf_op jit(solution)/shard_map/ppermute | solution.py:14
  48.1 4.0 %copy-start.3 = (bf16[256,256]{1,0:T(8,128)(2,1)}, bf16[256,256]{1,0:T(8,128)(2,1)S(1)}, u32[]{:S(2)}) copy-start(bf16[256,256]{1,0:T(8,128)(2,1)S(1)} %all-reduce.4) | copy-start | bytes 393220
  48.1 10.8 %copy-start.6 = (bf16[4,768,3072]{2,1,0:T(8,128)(2,1)S(1)}, bf16[4,768,3072]{2,1,0:T(8,128)(2,1)}, u32[]{:S(2)}) copy-start(bf16[4,768,3072]{2,1,0:T(8,128)(2,1)} %param.6) | copy-start | bytes 56623108
  58.9 3.1 %copy-start.7 = (bf16[256,3072]{1,0:T(8,128)(2,1)S(1)}, bf16[256,3072]{1,0:T(8,128)(2,1)}, u32[]{:S(2)}) copy-start(bf16[256,3072]{1,0:T(8,128)(2,1)} %param.9) | copy-start | bytes 4718596
  75.1 2.4 %copy-start.4 = (bf16[256,256]{1,0:T(8,128)(2,1)S(1)}, bf16[256,256]{1,0:T(8,128)(2,1)}, u32[]{:S(2)}) copy-start(bf16[256,256]{1,0:T(8,128)(2,1)} %copy-done.3) | copy-start | bytes 393220
  77.6 37.8 %copy-start.1 = (bf16[256,768]{1,0:T(8,128)(2,1)S(1)}, bf16[256,768]{1,0:T(8,128)(2,1)}, u32[]{:S(2)}) copy-start(bf16[256,768]{1,0:T(8,128)(2,1)} %param.5) | copy-start | bytes 1179652
  117.5 93.6 %collective-permute-start.3 = (f32[256,768]{1,0:T(8,128)}, f32[256,768]{1,0:T(8,128)}, u32[]{:S(2)}, u32[]{:S(2)}) collective-permute-start(f32[256,768]{1,0:T(8,128)} %fusion.8), channel_id=1, source_target_pairs={{0,1},{1,0},{2,3},{3,2},{4,5},{5,4},{6,7},{7,6},{8,9},{9,8},{10,11... | collective-permute-start | bytes 2359304 | tf_op jit(solution)/shard_map/ppermute | solution.py:14
  118.4 92.6 %collective-permute-start.4 = (f32[256,768]{1,0:T(8,128)}, f32[256,768]{1,0:T(8,128)}, u32[]{:S(2)}, u32[]{:S(2)}) collective-permute-start(f32[256,768]{1,0:T(8,128)} %fusion.4), channel_id=1, source_target_pairs={{0,2},{2,0},{1,3},{3,1},{4,6},{6,4},{5,7},{7,5},{8,10},{10,8},{9,1... | collective-permute-start | bytes 2359304 | tf_op jit(solution)/shard_map/ppermute | solution.py:14
  118.4 92.7 %collective-permute-start.5 = (f32[256,768]{1,0:T(8,128)}, f32[256,768]{1,0:T(8,128)}, u32[]{:S(2)}, u32[]{:S(2)}) collective-permute-start(f32[256,768]{1,0:T(8,128)} %fusion), channel_id=1, source_target_pairs={{0,4},{4,0},{1,5},{5,1},{2,6},{6,2},{3,7},{7,3},{8,12},{12,8},{9,1... | collective-permute-start | bytes 2359304 | tf_op jit(solution)/shard_map/ppermute | solution.py:14
  207.2 3.9 %copy-start.2 = (bf16[768,256]{1,0:T(8,128)(2,1)S(1)}, bf16[768,256]{1,0:T(8,128)(2,1)}, u32[]{:S(2)}) copy-start(bf16[768,256]{1,0:T(8,128)(2,1)} %param.7) | copy-start | bytes 1179652
  207.2 3.9 %copy-start.5 = (bf16[256,256]{1,0:T(8,128)(2,1)S(1)}, bf16[256,256]{1,0:T(8,128)(2,1)}, u32[]{:S(2)}) copy-start(bf16[256,256]{1,0:T(8,128)(2,1)} %all-reduce.5) | copy-start | bytes 393220
where the time goes:
time: 218 us; the launch traced here: 214 us
  blocking collectives  157 us (72%)
  matrix products  41.7 us (19%)
  starting transfers between devices  13.4 us (6%)
    psum x1, blocking collectives, body(): left_total, right_total = lax.psum((left_part, right_part), 'dp')  84 us
    psum x1, blocking collectives, body(): low_rank = lax.psum(low_part, 'tensor').astype(jnp.bfloat16)  37.5 us
    psum x1, blocking collectives, body(): mixed_rows = lax.psum(mixed_part, 'tensor').astype(jnp.bfloat16)  35.5 us
    dot_general x8, matrix products, across(): lax.dot_general(left, right, (((left_dim,), (right_dim,)), ((), ())), pre...  19.5 us
    dot_general x3, matrix products, body(): jnp.dot(partner, blocks[bit_index + 1], preferred_element_type=jnp.float32)  16.1 us
    ppermute x6, starting transfers between devices, partner_2(): return lax.ppermute(block, axis, route)  13.4 us
  transfers between devices with their start and end apart: 6, of which 0 were waited for; matrix products, arithmetic and copies ran while one was open for 9% of the time, Pallas kernels for 0%

commit v1 on v0

v1 whole, which is shorter than its diff:
```python
import functools

import jax
import jax.numpy as jnp
from jax import lax
from jax.experimental import pallas as pl
from jax.experimental.pallas import tpu as pltpu
from jax.sharding import PartitionSpec as P

MESH = pl.DeviceIdType.MESH
BF = jnp.bfloat16
F32 = jnp.float32
C0 = 0.7978845608028654
C1 = 0.044715

NC = 6
NK = 3


def flip(v, mask):
    for b in range(3):
        if mask >> b & 1:
            bit = lax.rem(lax.div(v, 1 << b), 2)
            v = v + (1 - 2 * bit) * (1 << b)
    return v


def mm(a, b):
    return jnp.dot(a, b, preferred_element_type=F32)


def mm_t(a, b):
    return lax.dot_general(a, b, (((1,), (1,)), ((), ())), preferred_element_type=F32)


def kernel(scale, sizes, tok_h, blk_h, lf_h, rf_h, up_h, act_h, tg_h, lg_h, rg_h,
           blk, tok, tok_t, lf, rf, up, act, pre, slo,
           lowf, lowp, low_rs, low, low_t,
           mixf, mixp, mix_rs, mix,
           gs, gr, own,
           rp, rpair, rps, ryr, rys, rxr, rg,
           lp, lpair, lps, l7r, lg,
           load_sem, out_sem, send_sem, recv_sem):
    rows, db, fb, rank = sizes
    cw, kw = fb // NC, db // NK
    part = rows // 8
    hr = rows // 2
    d = lax.axis_index("dp")
    t = lax.axis_index("tensor")
    core = lax.rem(d, 2)
    y = lax.rem(lax.div(d, 2), 4)
    xl = lax.div(d, 8)

    def dev(x, yy, c):
        return (x * 8 + yy * 2 + c, t)

    def peer(mask):
        return (d, flip(t, mask))

    pair = dev(xl, y, 1 - core)
    xpeer = dev(1 - xl, y, core)

    def ypeer(k):
        return dev(xl, lax.rem(y + k, 4), core)

    chips = [(k, f) for f in range(2) for k in range(4) if (k, f) != (0, 0)]

    def chip(k, f):
        return dev(xl if f == 0 else 1 - xl, lax.rem(y + k, 4), core)

    started = []

    def send(src, dst, to):
        i = len(started)
        c = pltpu.make_async_remote_copy(
            src_ref=src, dst_ref=dst, send_sem=send_sem.at[i], recv_sem=recv_sem.at[i],
            device_id=to, device_id_type=MESH)
        c.start()
        started.append(c)
        return c

    loads = []

    def load(src, dst):
        c = pltpu.make_async_copy(src, dst, load_sem.at[len(loads)])
        c.start()
        loads.append(c)
        return c

    outs = []

    def put(src, dst):
        c = pltpu.make_async_copy(src, dst, out_sem.at[len(outs)])
        c.start()
        outs.append(c)

    l_tok = load(tok_h, tok.at[0])
    l_lf = load(lf_h, lf)
    l_blk = [load(blk_h.at[0], blk.at[0])]
    l_rf = load(rf_h, rf)
    l_blk += [load(blk_h.at[s], blk.at[s]) for s in (2, 1)]
    l_blk += [load(blk_h.at[3], blk.at[3])]
    l_up = load(up_h, up)

    bar = pltpu.get_barrier_semaphore()
    peers = [peer(m) for m in range(1, 8)] + [pair] + [chip(k, f) for k, f in chips]
    for p in peers:
        pl.semaphore_signal(bar, inc=1, device_id=p, device_id_type=MESH)

    l_tok.wait()
    l_lf.wait()
    lowf[...] = mm(tok[0], lf[...])
    lowp[...] = lowf[...].astype(BF)
    pl.semaphore_wait(bar, len(peers))

    def scatter(src, dst):
        return [send(src.at[pl.ds(flip(t, m) * part, part)], dst.at[m - 1], peer(m))
                for m in range(1, 8)]

    def gather(buf):
        here = pl.ds(t * part, part)
        return [send(buf.at[here], buf.at[here], peer(m)) for m in range(1, 8)]

    def gather_sum(f32_ref, recv):
        here = pl.ds(t * part, part)
        total = f32_ref[here, :]
        for m in range(7):
            total = total + recv[m].astype(F32)
        return total.astype(BF)

    c_low = scatter(lowp, low_rs)
    quads = [(k, h) for k in range(NK) for h in range(2)]

    def piece(s, k, h):
        return tok.at[s, pl.ds(h * hr, hr), pl.ds(k * kw, kw)]

    c_z1, c_xh = [], []
    for k, h in quads:
        c_z1.append(send(piece(0, k, h), piece(2, k, h), peer(2)))
        c_xh.append(send(piece(0, k, h), piece(1, k, h), peer(1)))

    l_blk[0].wait()

    def col(c):
        return pl.ds(pl.multiple_of(c * cw, cw), cw)

    def own_step(c, _):
        pre[:, col(c)] = mm(tok[0], blk[0, :, col(c)])
        return 0

    lax.fori_loop(0, NC, own_step, 0, unroll=True)
    tok_t[...] = tok[0].astype(F32).T.astype(BF)

    c_z2 = []

    def relay(i):
        k, h = quads[i]
        c_z1[i].wait_recv()
        c_z2.append(send(piece(2, k, h), piece(3, k, h), peer(6)))

    def add_k(s, k):
        ks = pl.ds(k * kw, kw)

        def step(c, _):
            pre[:, col(c)] += mm(tok[s, :, ks], blk[s, ks, col(c)])
            return 0

        lax.fori_loop(0, NC, step, 0, unroll=True)

    relay(0)
    for c in c_low:
        c.wait_recv()
    low[pl.ds(t * part, part), :] = gather_sum(lowf, low_rs)
    c_low_ag = gather(low)
    relay(1)
    l_blk[1].wait()
    add_k(2, 0)
    relay(2)
    l_blk[2].wait()
    c_xh[0].wait_recv()
    c_xh[1].wait_recv()
    add_k(1, 0)
    relay(3)
    add_k(2, 1)
    relay(4)
    c_xh[2].wait_recv()
    c_xh[3].wait_recv()
    add_k(1, 1)
    relay(5)
    add_k(2, 2)
    l_blk[3].wait()
    c_z2[0].wait_recv()
    c_z2[1].wait_recv()
    add_k(3, 0)
    c_xh[4].wait_recv()
    c_xh[5].wait_recv()
    add_k(1, 2)
    l_rf.wait()
    for c in c_low_ag:
        c.wait_recv()
    low_t[...] = low[...].astype(F32).T.astype(BF)

    def low_step(c, _):
        pre[:, col(c)] += mm(low[...], rf[:, col(c)])
        return 0

    lax.fori_loop(0, NC, low_step, 0, unroll=True)
    c_z2[2].wait_recv()
    c_z2[3].wait_recv()
    add_k(3, 1)
    l_up.wait()
    c_z2[4].wait_recv()
    c_z2[5].wait_recv()

    q = rank // 8
    e = rank // 16
    half = rank // 2
    c_pair, c_y, c_x, c_ax, c_ay, c_ap = {}, {}, {}, {}, {}, {}
    base = core * half + y * q

    def r_pair(c):
        c_pair[c] = send(rp.at[c, pl.ds((1 - core) * half, half)], rpair.at[c], pair)

    def r_y(c):
        c_pair[c].wait_recv()
        rps[c] = (rp[c, pl.ds(core * half, half)].astype(F32) + rpair[c].astype(F32)).astype(BF)
        c_y[c] = [send(rps.at[c, pl.ds(lax.rem(y + k, 4) * q, q)], ryr.at[c, k - 1], ypeer(k))
                  for k in (2, 1, 3)]

    def r_x(c):
        for s in c_y[c]:
            s.wait_recv()
        total = rps[c, pl.ds(y * q, q)].astype(F32)
        for k in range(3):
            total = total + ryr[c, k].astype(F32)
        rys[c] = total.astype(BF)
        c_x[c] = send(rys.at[c, pl.ds((1 - xl) * e, e)], rxr.at[c], xpeer)

    def r_ax(c):
        c_x[c].wait_recv()
        total = rys[c, pl.ds(xl * e, e)].astype(F32) + rxr[c].astype(F32)
        here = pl.ds(base + xl * e, e)
        rg[c, here] = (total * scale).astype(BF)
        c_ax[c] = send(rg.at[c, here], rg.at[c, here], xpeer)

    def r_ay(c):
        c_ax[c].wait_recv()
        here = pl.ds(base, q)
        c_ay[c] = [send(rg.at[c, here], rg.at[c, here], ypeer(k)) for k in (2, 1, 3)]

    def r_ap(c):
        for s in c_ay[c]:
            s.wait_recv()
        here = pl.ds(core * half, half)
        c_ap[c] = send(rg.at[c, here], rg.at[c, here], pair)

    def r_out(c):
        c_ap[c].wait_recv()
        put(rg.at[c], rg_h.at[:, pl.ds(c * cw, cw)])

    last = pl.ds((NK - 1) * kw, kw)
    for c in range(NC):
        cs = pl.ds(c * cw, cw)
        v = pre[:, cs] + mm(tok[3, :, last], blk[3, last, cs])
        u = up[:, cs].astype(F32)
        v2 = v * v
        th = jnp.tanh(v * (C0 + (C0 * C1) * v2))
        g = 0.5 + 0.5 * th
        act[:, cs] = (v * g).astype(BF)
        slope = g + 0.5 * v * (1.0 - th * th) * (C0 + (3.0 * C0 * C1) * v2)
        sl = (u * slope).astype(BF)
        slo[:, cs] = sl
        put(act.at[:, cs], act_h.at[:, cs])
        rp[c] = mm(low_t[...], sl).astype(BF)
        r_pair(c)
        m = mm_t(sl, rf[:, cs])
        if c == 0:
            mixf[...] = m
        else:
            mixf[...] += m
        if c >= 3:
            r_y(c - 3)
    mixp[...] = mixf[...].astype(BF)
    c_mix = scatter(mixp, mix_rs)

    def back(s, k):
        return mm_t(slo[...], blk[s, pl.ds(k * kw, kw), :])

    def gcol(ref, i, k):
        return ref.at[i, :, pl.ds(k * kw, kw)]

    c_g2, c_gx, c_g1 = [], [], []
    for k in range(NK):
        gs[0, :, pl.ds(k * kw, kw)] = back(3, k).astype(BF)
        c_g2.append(send(gcol(gs, 0, k), gcol(gr, 0, k), peer(6)))
        r_y(NC - 3 + k)
    for k in range(NK):
        gs[1, :, pl.ds(k * kw, kw)] = back(1, k).astype(BF)
        c_gx.append(send(gcol(gs, 1, k), gcol(gr, 1, k), peer(1)))
    r_x(0)
    for c in c_mix:
        c.wait_recv()
    mix[pl.ds(t * part, part), :] = gather_sum(mixf, mix_rs)
    c_mix_ag = gather(mix)
    for k in range(NK):
        ks = pl.ds(k * kw, kw)
        p = back(2, k)
        c_g2[k].wait_recv()
        gs[2, :, ks] = (p + gr[0, :, ks].astype(F32)).astype(BF)
        c_g1.append(send(gcol(gs, 2, k), gcol(gr, 2, k), peer(2)))
        r_x(1 + k)
        r_ax(k)
    for k in range(NK):
        own[:, pl.ds(k * kw, kw)] = back(0, k)
    r_ay(0)
    r_x(4)
    r_ax(3)
    r_ay(1)

    for c in c_mix_ag:
        c.wait_recv()
    lp[...] = mm(tok_t[...], mix[...]).astype(BF)
    lh, le = db // 2, db // 16
    c_lpair = send(lp.at[pl.ds((1 - core) * lh, lh)], lpair, pair)
    r_ay(2)
    r_x(5)
    r_ax(4)
    c_lpair.wait_recv()
    lps[...] = (lp[pl.ds(core * lh, lh)].astype(F32) + lpair[...].astype(F32)).astype(BF)
    c_l7 = []
    for i, (k, f) in enumerate(chips):
        xx = xl if f == 0 else 1 - xl
        at = lax.rem(y + k, 4) * (2 * le) + xx * le
        c_l7.append(send(lps.at[pl.ds(at, le)], l7r.at[i], chip(k, f)))
    r_ay(3)
    r_ax(5)
    r_ap(0)
    r_ap(1)
    r_ay(4)
    for k in range(NK):
        own[:, pl.ds(k * kw, kw)] += mm_t(mix[...], lf[pl.ds(k * kw, kw), :])
    r_out(0)
    r_ap(2)
    for c in c_l7:
        c.wait_recv()
    total = lps[pl.ds(y * (2 * le) + xl * le, le)].astype(F32)
    for i in range(7):
        total = total + l7r[i].astype(F32)
    here = pl.ds(core * lh + y * (2 * le) + xl * le, le)
    lg[here] = (total * scale).astype(BF)
    c_lag = [send(lg.at[here], lg.at[here], chip(k, f)) for k, f in chips]
    r_ay(5)
    r_ap(3)
    for k in range(NK):
        ks = pl.ds(k * kw, kw)
        c_gx[k].wait_recv()
        c_g1[k].wait_recv()
        tok[1, :, ks] = (own[:, ks] + gr[1, :, ks].astype(F32) + gr[2, :, ks].astype(F32)).astype(BF)
    put(tok.at[1], tg_h)
    r_out(1)
    r_ap(4)
    r_out(2)
    for c in c_lag:
        c.wait_recv()
    here = pl.ds(core * lh, lh)
    c_lap = send(lg.at[here], lg.at[here], pair)
    r_ap(5)
    r_out(3)
    r_out(4)
    c_lap.wait_recv()
    put(lg, lg_h)
    r_out(5)
    for c in started:
        c.wait_send()
    for c in outs:
        c.wait()


def move(*refs):
    n = (len(refs) - 1) // 2
    sem = refs[-1]
    cs = [pltpu.make_async_copy(refs[i], refs[n + i], sem.at[i]) for i in range(n)]
    for c in cs:
        c.start()
    for c in cs:
        c.wait()


def body(scale, tokens, blocks, left_factor, right_factor, upstream):
    rows, db = tokens.shape
    ns, _, fb = blocks.shape
    rank = left_factor.shape[1]
    cw = fb // NC
    part = rows // 8
    shapes = [
        jax.ShapeDtypeStruct((rows, fb), BF),
        jax.ShapeDtypeStruct((rows, db), BF),
        jax.ShapeDtypeStruct((db, rank), BF),
        jax.ShapeDtypeStruct((rank, fb), BF),
    ]
    V = pltpu.VMEM
    scratch = [
        V((ns, db, fb), BF), V((ns, rows, db), BF), V((db, rows), BF), V((db, rank), BF),
        V((rank, fb), BF), V((rows, fb), BF), V((rows, fb), BF), V((rows, fb), F32), V((rows, fb), BF),
        V((rows, rank), F32), V((rows, rank), BF), V((7, part, rank), BF), V((rows, rank), BF), V((rank, rows), BF),
        V((rows, rank), F32), V((rows, rank), BF), V((7, part, rank), BF), V((rows, rank), BF),
        V((3, rows, db), BF), V((3, rows, db), BF), V((rows, db), F32),
        V((NC, rank, cw), BF), V((NC, rank // 2, cw), BF), V((NC, rank // 2, cw), BF),
        V((NC, 3, rank // 8, cw), BF), V((NC, rank // 8, cw), BF), V((NC, rank // 16, cw), BF), V((NC, rank, cw), BF),
        V((db, rank), BF), V((db // 2, rank), BF), V((db // 2, rank), BF), V((7, db // 16, rank), BF), V((db, rank), BF),
        pltpu.SemaphoreType.DMA((8,)), pltpu.SemaphoreType.DMA((16,)),
        pltpu.SemaphoreType.DMA((160,)), pltpu.SemaphoreType.DMA((160,)),
    ]
    any_spec = pl.BlockSpec(memory_space=pl.ANY)
    res = pl.pallas_call(
        functools.partial(kernel, scale, (rows, db, fb, rank)),
        out_shape=shapes,
        in_specs=[any_spec] * 5,
        out_specs=[any_spec] * 4,
        scratch_shapes=scratch,
        compiler_params=pltpu.CompilerParams(
            collective_id=0, has_side_effects=True, vmem_limit_bytes=56 * 1024 * 1024
        ),
    )(tokens, blocks, left_factor, right_factor, upstream)
    return pl.pallas_call(
        move,
        out_shape=shapes,
        in_specs=[any_spec] * 4,
        out_specs=[any_spec] * 4,
        scratch_shapes=[pltpu.SemaphoreType.DMA((4,))],
    )(*res)


def solution(mesh):
    placed = (
        P("dp", "tensor"),
        P(None, "tensor", None),
        P("tensor", None),
        P(None, "tensor"),
        P("dp", "tensor"),
    )

    def whole(tokens, blocks, left_factor, right_factor, upstream):
        scale = 1.0 / float(tokens.shape[0]) ** 0.5
        return jax.shard_map(
            functools.partial(body, scale),
            mesh=mesh,
            in_specs=placed,
            out_specs=(P("dp", "tensor"), P("dp", "tensor"), P("tensor", None), P(None, "tensor")),
            check_vma=False,
        )(tokens, blocks, left_factor, right_factor, upstream)

    return whole
```

time: 218 us -> 192 us (0.88); the launches traced: 214 us -> 192 us
  Pallas kernels: 0 us -> 191 us
  blocking collectives: 157 us -> 0 us
  matrix products: 41.7 us -> 0 us
  starting transfers between devices: 13.4 us -> 0 us
    pallas_call x0 -> x2, Pallas kernels: none -> 191 us  [the longest x1 120 us: body(): pl.pallas_call(move, out_shape=shapes, in_specs=[any_spec] * 4, out_specs...]
    psum x3 -> x0, blocking collectives: 157 us -> none  [the longest x1 84 us: body(): left_total, right_total = lax.psum((left_part, right_part), 'dp')]
    dot_general x14 -> x0, matrix products: 41.7 us -> none  [the longest x8 19.5 us: across(): lax.dot_general(left, right, (((left_dim,), (right_dim,)), ((), ())), pre...]
    ppermute x6 -> x0, starting transfers between devices: 13.4 us -> none  [partner_2(): return lax.ppermute(block, axis, route)]
  transfers between devices with their start and end apart: 6 -> 0, of which waited for: 0 -> 0; matrix products, arithmetic and copies ran while one was open for 9% -> 0% of each run, Pallas kernels for 0% -> 0%
where the time goes in v1:
time: 192 us
  Pallas kernels  191 us (99%)
    pallas_call x1, Pallas kernels, body(): pl.pallas_call(move, out_shape=shapes, in_specs=[any_spec] * 4, out_specs...  120 us
    pallas_call x1, Pallas kernels, body(): pl.pallas_call(functools.partial(kernel, scale, (rows, db, fb, rank)), ou...  70.6 us

profile of v1, /device:TPU:1, one launch (start us, length us, event | category | flops | bytes accessed | tf_op | source)
XLA Modules:
  0.0 191.7 jit_solution(4608674589819098089)
XLA Ops:
  0.6 70.6 %shard_map.84 = (bf16[256,3072]{1,0:T(8,128)(2,1)}, bf16[256,768]{1,0:T(8,128)(2,1)}, bf16[768,256]{1,0:T(8,128)(2,1)}, bf16[256,3072]{1,0:T(8,128)(2,1)}) custom-call(bf16[256,768]{1,0:T(8,128)(2,1)} %tok_h.1, bf16[4,768,3072]{2,1,0:T(8,128)(2,1)} %blk_h.1, bf16[768,256]{1,0:T(8,128)(2,1)} %lf_h.1, bf16[256,3072]{1,0:T(8,128)(2,1)} %rf_h.1, ...), custom_call_target="tpu_custom_call" | custom-call | tf_op jit(solution)/shard_map/pallas_call | solution.py:415
  71.3 120.3 %shard_map.85 = (bf16[256,3072]{1,0:T(8,128)(2,1)}, bf16[256,768]{1,0:T(8,128)(2,1)}, bf16[768,256]{1,0:T(8,128)(2,1)}, bf16[256,3072]{1,0:T(8,128)(2,1)}) custom-call(bf16[256,3072]{1,0:T(8,128)(2,1)} %get-tuple-element.8.refs_0_, bf16[256,768]{1,0:T(8,128)(2,1)} %get-tuple-element.9.refs_1_, bf16[768,256]{1,0:T(8,128)(2,1)} %get-tuple-element.10.refs_2_, ...), custom_call_target="tpu_custom_call" | custom-call | tf_op jit(solution)/shard_map/pallas_call | solution.py:425

commit v2 on v0

v2 whole, which is shorter than its diff:
```python
import functools

import jax
import jax.numpy as jnp
from jax import lax
from jax.experimental import pallas as pl
from jax.experimental.pallas import tpu as pltpu
from jax.sharding import PartitionSpec as P

MESH = pl.DeviceIdType.MESH
BF = jnp.bfloat16
F32 = jnp.float32
C0 = 0.7978845608028654
C1 = 0.044715

NC = 6
NG = 3
XF = (4, 5)
NK = 3


def flip(v, mask):
    for b in range(3):
        if mask >> b & 1:
            bit = lax.rem(lax.div(v, 1 << b), 2)
            v = v + (1 - 2 * bit) * (1 << b)
    return v


def mm(a, b):
    return jnp.dot(a, b, preferred_element_type=F32)


def mm_t(a, b):
    return lax.dot_general(a, b, (((1,), (1,)), ((), ())), preferred_element_type=F32)


def kernel(scale, sizes, tok_h, blk_h, lf_h, rf_h, up_h, act, tg, lg, rg,
           blk, tok, tok_t, lf, rf, up, pre, slo,
           lowf, lowp, low_rs, low, low_t,
           mixf, mixp, mix_rs, mix,
           gs, gr, own,
           rp, rpair, rps, ryr, rys, rxr, rxs,
           lp, lpair, lps, l7r,
           load_sem, send_sem, recv_sem):
    rows, db, fb, rank = sizes
    cw, kw, gw = fb // NC, db // NK, fb // NG
    part = rows // 8
    hr = rows // 2
    d = lax.axis_index("dp")
    t = lax.axis_index("tensor")
    core = lax.rem(d, 2)
    y = lax.rem(lax.div(d, 2), 4)
    xl = lax.div(d, 8)

    def dev(x, yy, c):
        return (x * 8 + yy * 2 + c, t)

    def peer(mask):
        return (d, flip(t, mask))

    def yat(k):
        return lax.rem(y + k, 4)

    pair = dev(xl, y, 1 - core)
    xpeer = dev(1 - xl, y, core)
    chips = [(k, f) for f in range(2) for k in (2, 1, 3, 0) if (k, f) != (0, 0)]

    def chip(k, f):
        return dev(xl if f == 0 else 1 - xl, yat(k), core)

    bar = pltpu.get_barrier_semaphore()
    peers = [peer(m) for m in (7, 5, 6, 4, 3, 1, 2)] + [chip(k, f) for k, f in chips] + [pair]
    for p in peers:
        pl.semaphore_signal(bar, inc=1, device_id=p, device_id_type=MESH)

    loads = []

    def load(src, dst):
        c = pltpu.make_async_copy(src, dst, load_sem.at[len(loads)])
        c.start()
        loads.append(c)
        return c

    l_tok = load(tok_h, tok.at[0])
    l_lf = load(lf_h, lf)
    l_blk = {}
    for i in (0, 2, 1, 3):
        l_blk[i] = load(blk_h.at[i], blk.at[i])
    l_rf = load(rf_h, rf)
    l_up = load(up_h, up)

    groups = []

    class Group:
        def __init__(self, copies, size):
            n = len(groups)
            if n >= N_SEND:
                groups[n - N_SEND].sent()
            self.ssem, self.rsem, self.size, self.open = send_sem.at[n % N_SEND], recv_sem.at[n], size, True
            groups.append(self)
            for src, dst, to in copies:
                pltpu.make_async_remote_copy(
                    src_ref=src, dst_ref=dst, send_sem=self.ssem, recv_sem=self.rsem,
                    device_id=to, device_id_type=MESH).start()

        def got(self):
            pltpu.make_async_copy(self.size, self.size, self.rsem).wait()

        def sent(self):
            if self.open:
                pltpu.make_async_copy(self.size, self.size, self.ssem).wait()
                self.open = False

    def send(src, dst, to):
        return Group([(src, dst, to)], src)

    def scatter(src, dst):
        return Group([(src.at[pl.ds(flip(t, m) * part, part)], dst.at[m - 1], peer(m)) for m in (7, 5, 6, 4, 3, 1, 2)], dst)

    def gather(buf):
        here = buf.at[pl.ds(t * part, part)]
        return Group([(here, here, peer(m)) for m in (7, 5, 6, 4, 3, 1, 2)], buf.at[pl.ds(0, 7 * part)])

    def gather_sum(f32_ref, recv):
        total = f32_ref[pl.ds(t * part, part), :]
        for m in range(7):
            total = total + recv[m].astype(F32)
        return total.astype(BF)

    def col(c):
        return pl.ds(pl.multiple_of(c * cw, cw), cw)

    def add_k(s, k):
        ks = pl.ds(k * kw, kw)

        def step(c, _):
            pre[:, col(c)] += mm(tok[s, :, ks], blk[s, ks, col(c)])
            return 0

        lax.fori_loop(0, NC, step, 0, unroll=True)

    quads = [(k, h) for k in range(NK) for h in range(2)]

    def piece(s, k, h):
        return tok.at[s, pl.ds(h * hr, hr), pl.ds(k * kw, kw)]

    c_z1, c_xh, c_z2 = [], [], []

    def send_tok(i):
        k, h = quads[i]
        c_z1.append(send(piece(0, k, h), piece(2, k, h), peer(2)))
        c_xh.append(send(piece(0, k, h), piece(1, k, h), peer(1)))

    def relay(i):
        k, h = quads[i]
        c_z1[i].got()
        c_z2.append(send(piece(2, k, h), piece(3, k, h), peer(6)))

    def own_fwd():
        l_blk[0].wait()

        def step(c, _):
            pre[:, col(c)] = mm(tok[0], blk[0, :, col(c)])
            return 0

        lax.fori_loop(0, NC, step, 0, unroll=True)
        tok_t[...] = tok[0].astype(F32).T.astype(BF)

    def low_fwd():
        low_t[...] = low[...].astype(F32).T.astype(BF)

        def step(c, _):
            pre[:, col(c)] += mm(low[...], rf[:, col(c)])
            return 0

        lax.fori_loop(0, NC, step, 0, unroll=True)

    st = {}

    def run(name, *a):
        with jax.named_scope(name + "".join("_%d" % i for i in a)):
            OPS[name](*a)

    def start():
        l_tok.wait()
        l_lf.wait()
        lowf[...] = mm(tok[0], lf[...])
        lowp[...] = lowf[...].astype(BF)

    def barrier():
        pl.semaphore_wait(bar, len(peers))

    def low_rs_send():
        st["low"] = scatter(lowp, low_rs)

    def low_ag_send():
        st["low"].got()
        low[pl.ds(t * part, part), :] = gather_sum(lowf, low_rs)
        st["low_ag"] = gather(low)

    def w_low():
        l_rf.wait()
        st["low_ag"].got()

    def w_blk(i):
        l_blk[i].wait()

    def w_xh(k):
        c_xh[2 * k].got()
        c_xh[2 * k + 1].got()

    def w_z2(k):
        c_z2[2 * k].got()
        c_z2[2 * k + 1].got()

    def gelu(c):
        if c == 0:
            l_up.wait()
        cs = pl.ds(c * gw, gw)
        v = pre[:, cs]
        u = up[:, cs].astype(F32)
        v2 = v * v
        th = jnp.tanh(v * (C0 + (C0 * C1) * v2))
        g = 0.5 + 0.5 * th
        act[:, cs] = (v * g).astype(BF)
        slope = g + 0.5 * v * (1.0 - th * th) * (C0 + (3.0 * C0 * C1) * v2)
        slo[:, cs] = (u * slope).astype(BF)
        n = NC // NG
        for i in range(n):
            rp[c * n + i] = mm(low_t[...], slo[:, pl.ds(c * gw + i * cw, cw)]).astype(BF)
        for i in range(n):
            r_pair(c * n + i)

    def mix_send():
        mixf[...] = mm_t(slo[...], rf[...])
        mixp[...] = mixf[...].astype(BF)
        st["mix"] = scatter(mixp, mix_rs)

    def mix_ag_send():
        st["mix"].got()
        mix[pl.ds(t * part, part), :] = gather_sum(mixf, mix_rs)
        st["mix_ag"] = gather(mix)

    half, q, e = rank // 2, rank // 8, rank // 16
    g = {}

    def rgc(c, at, n):
        return rg.at[pl.ds(at, n), pl.ds(c * cw, cw)]

    def first(c):
        return (xl * (half // 2), half // 2) if c in XF else (y * q, q)

    def mine(c):
        return core * half + (xl * (half // 2) + y * e if c in XF else y * q + xl * e)

    def r_pair(c):
        g["p", c] = send(rp.at[c, pl.ds((1 - core) * half, half)], rpair.at[c], pair)

    def r_s2(c):
        g["p", c].got()
        rps[c] = (rp[c, pl.ds(core * half, half)].astype(F32) + rpair[c].astype(F32)).astype(BF)
        if c in XF:
            n = half // 2
            g["s2", c] = send(rps.at[c, pl.ds((1 - xl) * n, n)], rxr.at[c, pl.ds(0, n)], xpeer)
        else:
            g["s2", c] = Group([(rps.at[c, pl.ds(yat(k) * q, q)], ryr.at[c, k - 1], (dev(xl, yat(k), core)))
                                for k in (2, 1, 3)], ryr.at[c])

    def r_s3(c):
        g["s2", c].got()
        if c in XF:
            n = half // 2
            rxs[c % 2] = (rps[c, pl.ds(xl * n, n)].astype(F32) + rxr[c, pl.ds(0, n)].astype(F32)).astype(BF)
            g["s3", c] = Group([(rxs.at[c % 2, pl.ds(yat(k) * e, e)], ryr.at[c, k - 1, pl.ds(0, e)], (dev(xl, yat(k), core)))
                                for k in (2, 1, 3)], rps.at[c, pl.ds(0, 3 * e)])
        else:
            total = rps[c, pl.ds(y * q, q)].astype(F32)
            for k in range(3):
                total = total + ryr[c, k].astype(F32)
            rys[c] = total.astype(BF)
            g["s3", c] = send(rys.at[c, pl.ds((1 - xl) * e, e)], rxr.at[c, pl.ds(0, e)], xpeer)

    def r_a1(c):
        g["s3", c].got()
        if c in XF:
            total = rxs[c % 2, pl.ds(y * e, e)].astype(F32)
            for k in range(3):
                total = total + ryr[c, k, pl.ds(0, e)].astype(F32)
        else:
            total = rys[c, pl.ds(xl * e, e)].astype(F32) + rxr[c, pl.ds(0, e)].astype(F32)
        rg[pl.ds(mine(c), e), pl.ds(c * cw, cw)] = (total * scale).astype(BF)
        here = rgc(c, mine(c), e)
        if c in XF:
            g["a1", c] = Group([(here, here, dev(xl, yat(k), core)) for k in (2, 1, 3)], rps.at[c, pl.ds(0, 3 * e)])
        else:
            g["a1", c] = send(here, here, xpeer)

    def r_a2(c):
        g["a1", c].got()
        at, n = first(c)
        here = rgc(c, core * half + at, n)
        if c in XF:
            g["a2", c] = send(here, here, xpeer)
        else:
            g["a2", c] = Group([(here, here, dev(xl, yat(k), core)) for k in (2, 1, 3)], ryr.at[c])

    def r_a3(c):
        g["a2", c].got()
        here = rgc(c, core * half, half)
        g["a3", c] = send(here, here, pair)

    def r_end(c):
        g["a3", c].got()

    def back(s):
        return mm_t(slo[...], blk[s])

    def gcol(ref, i, k, n=NK):
        w = db // n
        return ref.at[i, :, pl.ds(k * w, w)]

    NX = 6

    def p2():
        gs[0] = back(3).astype(BF)
        for k in range(NK):
            g["g2", k] = send(gcol(gs, 0, k), gcol(gr, 0, k), peer(6))

    def px():
        gs[1] = back(1).astype(BF)

    def px_send(k):
        g["gx", k] = send(gcol(gs, 1, k, NX), gcol(gr, 1, k, NX), peer(1))

    def p1():
        pre[:, pl.ds(0, db)] = back(2)

    def p1_send(k):
        ks = pl.ds(k * kw, kw)
        g["g2", k].got()
        gs[2, :, ks] = (pre[:, ks] + gr[0, :, ks].astype(F32)).astype(BF)
        g["g1", k] = send(gcol(gs, 2, k), gcol(gr, 2, k), peer(2))

    def p0():
        own[...] = back(0)

    lh, le = db // 2, db // 16

    def left(i=0):
        st["mix_ag"].got()
        lp[...] = mm(tok_t[...], mix[...]).astype(BF)
        g["lp"] = send(lp.at[pl.ds((1 - core) * lh, lh)], lpair, pair)
        own[...] += mm_t(mix[...], lf[...])

    def left_rs():
        g["lp"].got()
        lps[...] = (lp[pl.ds(core * lh, lh)].astype(F32) + lpair[...].astype(F32)).astype(BF)
        cs = []
        for i, (k, f) in enumerate(chips):
            xx = xl if f == 0 else 1 - xl
            cs.append((lps.at[pl.ds(yat(k) * (2 * le) + xx * le, le)], l7r.at[i], chip(k, f)))
        g["l7"] = Group(cs, l7r)

    def left_ag():
        g["l7"].got()
        at = y * (2 * le) + xl * le
        total = lps[pl.ds(at, le)].astype(F32)
        for i in range(7):
            total = total + l7r[i].astype(F32)
        lg[pl.ds(core * lh + at, le)] = (total * scale).astype(BF)
        here = lg.at[pl.ds(core * lh + at, le)]
        g["la"] = Group([(here, here, chip(k, f)) for k, f in chips], l7r)

    def left_pair():
        g["la"].got()
        here = lg.at[pl.ds(core * lh, lh)]
        g["lap"] = send(here, here, pair)

    def left_end():
        g["lap"].got()

    def tg_end():
        for k in range(NX):
            g["gx", k].got()
        for k in range(NK):
            g["g1", k].got()
        tg[...] = (own[...] + gr[1].astype(F32) + gr[2].astype(F32)).astype(BF)

    def finish():
        for c in groups:
            c.sent()

    OPS = dict(locals())
    for name, *a in ORDER:
        run(name, *a)


ORDER = [
    ("start",), ("barrier",), ("send_tok", 0), ("low_rs_send",),
    *[("send_tok", i) for i in range(1, 6)],
    ("own_fwd",),
    ("relay", 0), ("relay", 1), ("low_ag_send",), ("w_blk", 2), ("add_k", 2, 0),
    ("relay", 2), ("w_blk", 1), ("w_xh", 0), ("add_k", 1, 0), ("relay", 3), ("add_k", 2, 1),
    ("relay", 4), ("w_xh", 1), ("add_k", 1, 1), ("relay", 5), ("add_k", 2, 2),
    ("w_blk", 3), ("w_z2", 0), ("add_k", 3, 0), ("w_xh", 2), ("add_k", 1, 2),
    ("w_low",), ("low_fwd",), ("w_z2", 1), ("add_k", 3, 1), ("w_z2", 2), ("add_k", 3, 2),
    ("gelu", 0), ("gelu", 1), ("gelu", 2),
    ("r_s2", 0), ("r_s2", 1), ("mix_send",), ("r_s2", 2), ("r_s2", 3), ("p2",), ("r_s2", 4), ("r_s2", 5),
    ("px",), ("px_send", 0), ("p1",), ("r_s3", 0), ("px_send", 1), ("mix_ag_send",), ("r_s3", 1), ("px_send", 2),
    ("r_s3", 4), ("r_s3", 5), ("p0",), ("r_a1", 0), ("p1_send", 0), ("r_s3", 2), ("px_send", 3),
    ("r_s3", 3), ("r_a1", 1), ("px_send", 4), ("p1_send", 1), ("r_a2", 0), ("r_a1", 2), ("px_send", 5),
    ("left",), ("r_a2", 1), ("r_a1", 3), ("p1_send", 2), ("left_rs",), ("r_a2", 2),
    ("r_a1", 4), ("r_a1", 5), ("r_a2", 3), ("r_a3", 0), ("r_a3", 1), ("r_a2", 4), ("r_a2", 5),
    ("left_ag",), ("r_a3", 2), ("tg_end",), ("r_a3", 3), ("r_a3", 4), ("r_a3", 5), ("left_pair",),
    *[("r_end", i) for i in range(6)], ("left_end",), ("finish",),
]
N_SEND = 20
N_RECV = 90


def move(*refs):
    n = len(refs) // 2
    sem = refs[-1]
    cs = [pltpu.make_async_copy(refs[i], refs[n + i], sem.at[i]) for i in range(n)]
    for c in cs:
        c.start()
    for c in cs:
        c.wait()


def body(scale, tokens, blocks, left_factor, right_factor, upstream):
    rows, db = tokens.shape
    ns, _, fb = blocks.shape
    rank = left_factor.shape[1]
    cw = fb // NC
    part = rows // 8
    shapes = [
        jax.ShapeDtypeStruct((rows, fb), BF),
        jax.ShapeDtypeStruct((rows, db), BF),
        jax.ShapeDtypeStruct((db, rank), BF),
        jax.ShapeDtypeStruct((rank, fb), BF),
    ]
    V = pltpu.VMEM
    scratch = [
        V((ns, db, fb), BF), V((ns, rows, db), BF), V((db, rows), BF), V((db, rank), BF),
        V((rank, fb), BF), V((rows, fb), BF), V((rows, fb), F32), V((rows, fb), BF),
        V((rows, rank), F32), V((rows, rank), BF), V((7, part, rank), BF), V((rows, rank), BF), V((rank, rows), BF),
        V((rows, rank), F32), V((rows, rank), BF), V((7, part, rank), BF), V((rows, rank), BF),
        V((3, rows, db), BF), V((3, rows, db), BF), V((rows, db), F32),
        V((NC, rank, cw), BF), V((NC, rank // 2, cw), BF), V((NC, rank // 2, cw), BF),
        V((NC, 3, rank // 8, cw), BF), V((NC, rank // 8, cw), BF), V((NC, rank // 4, cw), BF), V((2, rank // 4, cw), BF),
        V((db, rank), BF), V((db // 2, rank), BF), V((db // 2, rank), BF), V((7, db // 16, rank), BF),
        pltpu.SemaphoreType.DMA((8,)), pltpu.SemaphoreType.DMA((N_SEND,)), pltpu.SemaphoreType.DMA((N_RECV,)),
    ]
    any_spec = pl.BlockSpec(memory_space=pl.ANY)
    vmem_spec = pl.BlockSpec(memory_space=pltpu.VMEM)
    res = pl.pallas_call(
        functools.partial(kernel, scale, (rows, db, fb, rank)),
        out_shape=[V(o.shape, o.dtype) for o in shapes],
        in_specs=[any_spec] * 5,
        out_specs=[vmem_spec] * 4,
        scratch_shapes=scratch,
        compiler_params=pltpu.CompilerParams(
            collective_id=0, has_side_effects=True, vmem_limit_bytes=56 * 1024 * 1024
        ),
    )(tokens, blocks, left_factor, right_factor, upstream)
    return pl.pallas_call(
        move,
        out_shape=shapes,
        in_specs=[vmem_spec] * 4,
        out_specs=[any_spec] * 4,
        scratch_shapes=[pltpu.SemaphoreType.DMA((4,))],
        compiler_params=pltpu.CompilerParams(vmem_limit_bytes=1024 * 1024),
    )(*[pltpu.with_memory_space_constraint(r, pltpu.VMEM) for r in res])


def solution(mesh):
    placed = (
        P("dp", "tensor"),
        P(None, "tensor", None),
        P("tensor", None),
        P(None, "tensor"),
        P("dp", "tensor"),
    )

    def whole(tokens, blocks, left_factor, right_factor, upstream):
        scale = 1.0 / float(tokens.shape[0]) ** 0.5
        return jax.shard_map(
            functools.partial(body, scale),
            mesh=mesh,
            in_specs=placed,
            out_specs=(P("dp", "tensor"), P("dp", "tensor"), P("tensor", None), P(None, "tensor")),
            check_vma=False,
        )(tokens, blocks, left_factor, right_factor, upstream)

    return whole
```

time: 218 us -> 65.1 us (0.30); the launches traced: 214 us -> 65 us
  blocking collectives: 157 us -> 0 us
  Pallas kernels: 0 us -> 64.2 us
  matrix products: 41.7 us -> 0 us
  starting transfers between devices: 13.4 us -> 0 us
    psum x3 -> x0, blocking collectives: 157 us -> none  [the longest x1 84 us: body(): left_total, right_total = lax.psum((left_part, right_part), 'dp')]
    pallas_call x0 -> x2, Pallas kernels: none -> 64.2 us  [the longest x1 62.2 us: body(): pl.pallas_call(functools.partial(kernel, scale, (rows, db, fb, rank)), ou...]
    dot_general x14 -> x0, matrix products: 41.7 us -> none  [the longest x8 19.5 us: across(): lax.dot_general(left, right, (((left_dim,), (right_dim,)), ((), ())), pre...]
    ppermute x6 -> x0, starting transfers between devices: 13.4 us -> none  [partner_2(): return lax.ppermute(block, axis, route)]
  transfers between devices with their start and end apart: 6 -> 0, of which waited for: 0 -> 0; matrix products, arithmetic and copies ran while one was open for 9% -> 0% of each run, Pallas kernels for 0% -> 0%
where the time goes in v2:
time: 65.1 us; the launch traced here: 65 us
  Pallas kernels  64.2 us (99%)
  between operations  0.8 us (1%)
    pallas_call x1, Pallas kernels, body(): pl.pallas_call(functools.partial(kernel, scale, (rows, db, fb, rank)), ou...  62.2 us
    pallas_call x1, Pallas kernels, body(): pl.pallas_call(move, out_shape=shapes, in_specs=[vmem_spec] * 4, out_spec...  1.96 us

profile of v2, /device:TPU:1, one launch (start us, length us, event | category | flops | bytes accessed | tf_op | source)
XLA Modules:
  0.0 65.0 jit_solution(740854051858544170)
XLA Ops:
  0.6 62.2 %shard_map.84 = (bf16[256,3072]{1,0:T(8,128)(2,1)S(1)}, bf16[256,768]{1,0:T(8,128)(2,1)S(1)}, bf16[768,256]{1,0:T(8,128)(2,1)S(1)}, bf16[256,3072]{1,0:T(8,128)(2,1)S(1)}) custom-call(bf16[256,768]{1,0:T(8,128)(2,1)} %tok_h.1, bf16[4,768,3072]{2,1,0:T(8,128)(2,1)} %blk_h.1, bf16[768,256]{1,0:T(8,128)(2,1)} %lf_h.1, bf16[256,3072]{1,0:T(8,128)(2,1)} %rf_h.1, ...), custom_call_target="tpu_custom_call" | custom-call | tf_op jit(solution)/shard_map/pallas_call | solution.py:458
  62.9 2.0 %shard_map.85 = (bf16[256,3072]{1,0:T(8,128)(2,1)}, bf16[256,768]{1,0:T(8,128)(2,1)}, bf16[768,256]{1,0:T(8,128)(2,1)}, bf16[256,3072]{1,0:T(8,128)(2,1)}) custom-call(bf16[256,3072]{1,0:T(8,128)(2,1)S(1)} %get-tuple-element.8.refs_0_, bf16[256,768]{1,0:T(8,128)(2,1)S(1)} %get-tuple-element.9.refs_1_, bf16[768,256]{1,0:T(8,128)(2,1)S(1)} %get-tuple-element.10.refs_2_, ...), custom_call_target="tpu_custom_call" | custom-call | tf_op jit(solution)/shard_map/pallas_call | solution.py:468

commit v3 on v2

--- a/solution.py
+++ b/solution.py
@@ -15,7 +15,6 @@
 
 NC = 6
 NG = 3
-XF = (4, 5)
 NK = 3
 
 
@@ -39,14 +38,13 @@
            blk, tok, tok_t, lf, rf, up, pre, slo,
            lowf, lowp, low_rs, low, low_t,
            mixf, mixp, mix_rs, mix,
-           gs, gr, own,
-           rp, rpair, rps, ryr, rys, rxr, rxs,
+           rb, gs, gr, own,
+           rp, rpair, rps, yrl, yfin, ybs, yb, rys, rxr,
            lp, lpair, lps, l7r,
            load_sem, send_sem, recv_sem):
     rows, db, fb, rank = sizes
     cw, kw, gw = fb // NC, db // NK, fb // NG
     part = rows // 8
-    hr = rows // 2
     d = lax.axis_index("dp")
     t = lax.axis_index("tensor")
     core = lax.rem(d, 2)
@@ -113,7 +111,7 @@
                 self.open = False
 
     def send(src, dst, to):
-        return Group([(src, dst, to)], src)
+        return Group([(src, dst, to)], dst)
 
     def scatter(src, dst):
         return Group([(src.at[pl.ds(flip(t, m) * part, part)], dst.at[m - 1], peer(m)) for m in (7, 5, 6, 4, 3, 1, 2)], dst)
@@ -140,17 +138,30 @@
 
         lax.fori_loop(0, NC, step, 0, unroll=True)
 
-    quads = [(k, h) for k in range(NK) for h in range(2)]
+    hr = rows // NH
+    quads = [(k, h) for k in range(NK) for h in range(NH)]
 
     def piece(s, k, h):
         return tok.at[s, pl.ds(h * hr, hr), pl.ds(k * kw, kw)]
 
-    c_z1, c_xh, c_z2 = [], [], []
-
-    def send_tok(i):
+    c_z1, c_xh, c_z2, c_b, c_z2b = [], [], [], [], []
+
+    def send_z(i):
         k, h = quads[i]
-        c_z1.append(send(piece(0, k, h), piece(2, k, h), peer(2)))
-        c_xh.append(send(piece(0, k, h), piece(1, k, h), peer(1)))
+        c_z1.append(send(tok_h.at[pl.ds(h * hr, hr), pl.ds(k * kw, kw)], piece(2, k, h), peer(2)))
+
+    def send_x(k):
+        ks = pl.ds(k * kw, kw)
+        c_xh.append(send(tok_h.at[:, ks], tok.at[1, :, ks], peer(1)))
+
+    def send_b(j):
+        k, h = quads[NB + j]
+        c_b.append(send(tok_h.at[pl.ds(h * hr, hr), pl.ds(k * kw, kw)], rb.at[j], peer(6)))
+
+    def relay_b(j):
+        k, h = quads[NB + j]
+        c_b[j].got()
+        c_z2b.append(send(rb.at[j], piece(3, k, h), peer(2)))
 
     def relay(i):
         k, h = quads[i]
@@ -169,12 +180,6 @@
 
     def low_fwd():
         low_t[...] = low[...].astype(F32).T.astype(BF)
-
-        def step(c, _):
-            pre[:, col(c)] += mm(low[...], rf[:, col(c)])
-            return 0
-
-        lax.fori_loop(0, NC, step, 0, unroll=True)
 
     st = {}
 
@@ -206,19 +211,22 @@
     def w_blk(i):
         l_blk[i].wait()
 
+    def w_z1(i):
+        c_z1[i].got()
+
     def w_xh(k):
-        c_xh[2 * k].got()
-        c_xh[2 * k + 1].got()
+        c_xh[k].got()
 
     def w_z2(k):
-        c_z2[2 * k].got()
-        c_z2[2 * k + 1].got()
+        for i in range(NH * k, NH * k + NH):
+            (c_z2[i] if i < NB else c_z2b[i - NB]).got()
 
     def gelu(c):
         if c == 0:
             l_up.wait()
         cs = pl.ds(c * gw, gw)
-        v = pre[:, cs]
+        last = pl.ds((NK - 1) * kw, kw)
+        v = pre[:, cs] + mm(tok[3, :, last], blk[3, last, cs]) + mm(low[...], rf[:, cs])
         u = up[:, cs].astype(F32)
         v2 = v * v
         th = jnp.tanh(v * (C0 + (C0 * C1) * v2))
@@ -227,13 +235,17 @@
         slope = g + 0.5 * v * (1.0 - th * th) * (C0 + (3.0 * C0 * C1) * v2)
         slo[:, cs] = (u * slope).astype(BF)
         n = NC // NG
-        for i in range(n):
-            rp[c * n + i] = mm(low_t[...], slo[:, pl.ds(c * gw + i * cw, cw)]).astype(BF)
-        for i in range(n):
-            r_pair(c * n + i)
+        for i in range(c * n, c * n + n):
+            rp[i] = mm(low_t[...], slo[:, pl.ds(i * cw, cw)]).astype(BF)
+        m = mm_t(slo[:, cs], rf[:, cs])
+        if c == 0:
+            mixf[...] = m
+        else:
+            mixf[...] += m
+        for i in range(c * n, c * n + n):
+            r_pair(i)
 
     def mix_send():
-        mixf[...] = mm_t(slo[...], rf[...])
         mixp[...] = mixf[...].astype(BF)
         st["mix"] = scatter(mixp, mix_rs)
 
@@ -244,15 +256,13 @@
 
     half, q, e = rank // 2, rank // 8, rank // 16
     g = {}
+    up_y, dn_y = dev(xl, yat(1), core), dev(xl, yat(3), core)
 
     def rgc(c, at, n):
         return rg.at[pl.ds(at, n), pl.ds(c * cw, cw)]
 
-    def first(c):
-        return (xl * (half // 2), half // 2) if c in XF else (y * q, q)
-
-    def mine(c):
-        return core * half + (xl * (half // 2) + y * e if c in XF else y * q + xl * e)
+    def rq(c, k, h):
+        return pl.ds(yat(k) * q + h * e, e)
 
     def r_pair(c):
         g["p", c] = send(rp.at[c, pl.ds((1 - core) * half, half)], rpair.at[c], pair)
@@ -260,61 +270,43 @@
     def r_s2(c):
         g["p", c].got()
         rps[c] = (rp[c, pl.ds(core * half, half)].astype(F32) + rpair[c].astype(F32)).astype(BF)
-        if c in XF:
-            n = half // 2
-            g["s2", c] = send(rps.at[c, pl.ds((1 - xl) * n, n)], rxr.at[c, pl.ds(0, n)], xpeer)
-        else:
-            g["s2", c] = Group([(rps.at[c, pl.ds(yat(k) * q, q)], ryr.at[c, k - 1], (dev(xl, yat(k), core)))
-                                for k in (2, 1, 3)], ryr.at[c])
+        g["yr", c] = Group([(rps.at[c, rq(c, 2, 0)], yrl.at[c, 0], up_y), (rps.at[c, rq(c, 2, 1)], yrl.at[c, 1], dn_y)], yrl.at[c])
+        g["yf", c] = Group([(rps.at[c, rq(c, 1, 1)], yfin.at[c, 1], up_y), (rps.at[c, rq(c, 3, 0)], yfin.at[c, 0], dn_y)], yfin.at[c])
+
+    def r_s2b(c):
+        g["yr", c].got()
+        ybs[c, 0] = (rps[c, rq(c, 1, 0)].astype(F32) + yrl[c, 0].astype(F32)).astype(BF)
+        ybs[c, 1] = (rps[c, rq(c, 3, 1)].astype(F32) + yrl[c, 1].astype(F32)).astype(BF)
+        g["yb", c] = Group([(ybs.at[c, 0], yb.at[c, 0], up_y), (ybs.at[c, 1], yb.at[c, 1], dn_y)], yb.at[c])
 
     def r_s3(c):
-        g["s2", c].got()
-        if c in XF:
-            n = half // 2
-            rxs[c % 2] = (rps[c, pl.ds(xl * n, n)].astype(F32) + rxr[c, pl.ds(0, n)].astype(F32)).astype(BF)
-            g["s3", c] = Group([(rxs.at[c % 2, pl.ds(yat(k) * e, e)], ryr.at[c, k - 1, pl.ds(0, e)], (dev(xl, yat(k), core)))
-                                for k in (2, 1, 3)], rps.at[c, pl.ds(0, 3 * e)])
-        else:
-            total = rps[c, pl.ds(y * q, q)].astype(F32)
-            for k in range(3):
-                total = total + ryr[c, k].astype(F32)
-            rys[c] = total.astype(BF)
-            g["s3", c] = send(rys.at[c, pl.ds((1 - xl) * e, e)], rxr.at[c, pl.ds(0, e)], xpeer)
-
-    def r_a1(c):
+        g["yf", c].got()
+        g["yb", c].got()
+        for h in range(2):
+            total = rps[c, rq(c, 0, h)].astype(F32) + yfin[c, h].astype(F32) + yb[c, h].astype(F32)
+            rys[c, pl.ds(h * e, e)] = total.astype(BF)
+        g["s3", c] = send(rys.at[c], rxr.at[c], xpeer)
+
+    def r_a2(c):
         g["s3", c].got()
-        if c in XF:
-            total = rxs[c % 2, pl.ds(y * e, e)].astype(F32)
-            for k in range(3):
-                total = total + ryr[c, k, pl.ds(0, e)].astype(F32)
-        else:
-            total = rys[c, pl.ds(xl * e, e)].astype(F32) + rxr[c, pl.ds(0, e)].astype(F32)
-        rg[pl.ds(mine(c), e), pl.ds(c * cw, cw)] = (total * scale).astype(BF)
-        here = rgc(c, mine(c), e)
-        if c in XF:
-            g["a1", c] = Group([(here, here, dev(xl, yat(k), core)) for k in (2, 1, 3)], rps.at[c, pl.ds(0, 3 * e)])
-        else:
-            g["a1", c] = send(here, here, xpeer)
-
-    def r_a2(c):
-        g["a1", c].got()
-        at, n = first(c)
-        here = rgc(c, core * half + at, n)
-        if c in XF:
-            g["a2", c] = send(here, here, xpeer)
-        else:
-            g["a2", c] = Group([(here, here, dev(xl, yat(k), core)) for k in (2, 1, 3)], ryr.at[c])
+        at = core * half + y * q
+        rg[pl.ds(at, q), pl.ds(c * cw, cw)] = ((rys[c].astype(F32) + rxr[c].astype(F32)) * scale).astype(BF)
+        here = rgc(c, at, q)
+        g["a2", c] = Group([(here, here, up_y), (here, here, dn_y)], rps.at[c, pl.ds(0, 2 * q)])
+
+    def r_a2b(c):
+        g["a2", c].got()
+        one = rgc(c, core * half + yat(3) * q, e)
+        two = rgc(c, core * half + yat(1) * q + e, e)
+        g["a2b", c] = Group([(one, one, up_y), (two, two, dn_y)], yb.at[c])
 
     def r_a3(c):
-        g["a2", c].got()
+        g["a2b", c].got()
         here = rgc(c, core * half, half)
         g["a3", c] = send(here, here, pair)
 
     def r_end(c):
         g["a3", c].got()
-
-    def back(s):
-        return mm_t(slo[...], blk[s])
 
     def gcol(ref, i, k, n=NK):
         w = db // n
@@ -322,35 +314,43 @@
 
     NX = 6
 
-    def p2():
-        gs[0] = back(3).astype(BF)
-        for k in range(NK):
-            g["g2", k] = send(gcol(gs, 0, k), gcol(gr, 0, k), peer(6))
-
-    def px():
-        gs[1] = back(1).astype(BF)
+    def p2(k):
+        ks = pl.ds(k * kw, kw)
+        gs[0, :, ks] = mm_t(slo[...], blk[3, ks, :]).astype(BF)
+
+    def p2_send(k):
+        g["g2", k] = send(gcol(gs, 0, k, NX), gcol(gr, 0, k, NX), peer(6))
+
+    def px(k):
+        ks = pl.ds(k * kw, kw)
+        gs[1, :, ks] = mm_t(slo[...], blk[1, ks, :]).astype(BF)
 
     def px_send(k):
         g["gx", k] = send(gcol(gs, 1, k, NX), gcol(gr, 1, k, NX), peer(1))
 
-    def p1():
-        pre[:, pl.ds(0, db)] = back(2)
+    def p1(k):
+        ks = pl.ds(k * kw, kw)
+        pre[:, ks] = mm_t(slo[...], blk[2, ks, :])
 
     def p1_send(k):
         ks = pl.ds(k * kw, kw)
-        g["g2", k].got()
+        g["g2", 2 * k].got()
+        g["g2", 2 * k + 1].got()
         gs[2, :, ks] = (pre[:, ks] + gr[0, :, ks].astype(F32)).astype(BF)
         g["g1", k] = send(gcol(gs, 2, k), gcol(gr, 2, k), peer(2))
 
-    def p0():
-        own[...] = back(0)
+    def p0(k):
+        ks = pl.ds(k * kw, kw)
+        own[:, ks] = mm_t(slo[...], blk[0, ks, :])
 
     lh, le = db // 2, db // 16
 
-    def left(i=0):
+    def left():
         st["mix_ag"].got()
         lp[...] = mm(tok_t[...], mix[...]).astype(BF)
         g["lp"] = send(lp.at[pl.ds((1 - core) * lh, lh)], lpair, pair)
+
+    def tg_low():
         own[...] += mm_t(mix[...], lf[...])
 
     def left_rs():
@@ -397,36 +397,44 @@
 
 
 ORDER = [
-    ("start",), ("barrier",), ("send_tok", 0), ("low_rs_send",),
-    *[("send_tok", i) for i in range(1, 6)],
-    ("own_fwd",),
-    ("relay", 0), ("relay", 1), ("low_ag_send",), ("w_blk", 2), ("add_k", 2, 0),
-    ("relay", 2), ("w_blk", 1), ("w_xh", 0), ("add_k", 1, 0), ("relay", 3), ("add_k", 2, 1),
-    ("relay", 4), ("w_xh", 1), ("add_k", 1, 1), ("relay", 5), ("add_k", 2, 2),
-    ("w_blk", 3), ("w_z2", 0), ("add_k", 3, 0), ("w_xh", 2), ("add_k", 1, 2),
-    ("w_low",), ("low_fwd",), ("w_z2", 1), ("add_k", 3, 1), ("w_z2", 2), ("add_k", 3, 2),
-    ("gelu", 0), ("gelu", 1), ("gelu", 2),
-    ("r_s2", 0), ("r_s2", 1), ("mix_send",), ("r_s2", 2), ("r_s2", 3), ("p2",), ("r_s2", 4), ("r_s2", 5),
-    ("px",), ("px_send", 0), ("p1",), ("r_s3", 0), ("px_send", 1), ("mix_ag_send",), ("r_s3", 1), ("px_send", 2),
-    ("r_s3", 4), ("r_s3", 5), ("p0",), ("r_a1", 0), ("p1_send", 0), ("r_s3", 2), ("px_send", 3),
-    ("r_s3", 3), ("r_a1", 1), ("px_send", 4), ("p1_send", 1), ("r_a2", 0), ("r_a1", 2), ("px_send", 5),
-    ("left",), ("r_a2", 1), ("r_a1", 3), ("p1_send", 2), ("left_rs",), ("r_a2", 2),
-    ("r_a1", 4), ("r_a1", 5), ("r_a2", 3), ("r_a3", 0), ("r_a3", 1), ("r_a2", 4), ("r_a2", 5),
-    ("left_ag",), ("r_a3", 2), ("tg_end",), ("r_a3", 3), ("r_a3", 4), ("r_a3", 5), ("left_pair",),
+    ("start",), ("barrier",), ("send_z", 0), ("send_b", 0), ("low_rs_send",), ("send_z", 1), ("send_x", 0), ("send_b", 1),
+    *[("send_z", i) for i in range(2, 8)], ("send_x", 1), *[("send_z", i) for i in range(8, 12)], ("send_x", 2), ("own_fwd",),
+    ("relay", 0), ("relay_b", 0), ("relay", 1), ("relay", 2), ("relay_b", 1), ("low_ag_send",), ("relay", 3), ("w_blk", 1), ("w_blk", 2),
+    ("add_k", 2, 0), ("relay", 4), ("relay", 5), ("w_xh", 0), ("add_k", 1, 0), ("relay", 6), ("relay", 7),
+    ("add_k", 2, 1), ("relay", 8), ("relay", 9), ("w_xh", 1), ("add_k", 1, 1), ("w_z1", 10), ("w_z1", 11),
+    ("add_k", 2, 2), ("w_blk", 3), ("w_z2", 0), ("add_k", 3, 0), ("w_xh", 2), ("add_k", 1, 2),
+    ("w_z2", 1), ("add_k", 3, 1), ("w_low",), ("low_fwd",), ("w_z2", 2),
+    ("gelu", 0), ("gelu", 1), ("r_s2", 0), ("r_s2", 1), ("gelu", 2), ("mix_send",), ("r_s2", 2), ("r_s2", 3),
+    ("px", 0), ("px_send", 0), ("px_send", 1), ("r_s2", 4), ("r_s2", 5), ("r_s2b", 0), ("r_s2b", 1), ("px", 1), ("r_s2b", 2), ("r_s2b", 3),
+    ("px", 2), ("mix_ag_send",), ("r_s2b", 4), ("r_s2b", 5), ("r_s3", 0), ("r_s3", 1), ("px_send", 2), ("p2", 0), ("p2_send", 0), ("p2_send", 1),
+    ("r_s3", 2), ("r_s3", 3), ("p2", 1), ("p2_send", 2), ("p2_send", 3), ("r_s3", 4), ("r_s3", 5), ("r_a2", 0), ("left",), ("r_a2", 1), ("p2", 2), ("p2_send", 4), ("p2_send", 5),
+    ("px_send", 3), ("left_rs",), ("r_a2", 2), ("r_a2", 3), ("r_a2b", 0), ("p1", 0), ("p1_send", 0), ("px_send", 4), ("r_a2", 4), ("r_a2b", 1), ("r_a2", 5),
+    ("p1", 1), ("p1_send", 1), ("px_send", 5), ("p1", 2), ("p1_send", 2), ("r_a2b", 2), ("p0", 0), ("r_a2b", 3), ("r_a3", 0), ("left_ag",), ("p0", 1), ("r_a2b", 4), ("r_a3", 1), ("r_a2b", 5), ("p0", 2), ("r_a3", 2),
+    ("r_a3", 3), ("tg_low",), ("r_a3", 4), ("left_pair",), ("r_a3", 5), ("tg_end",),
     *[("r_end", i) for i in range(6)], ("left_end",), ("finish",),
 ]
+NB = 10
+NH = 4
 N_SEND = 20
-N_RECV = 90
+N_RECV = 100
 
 
 def move(*refs):
     n = len(refs) // 2
     sem = refs[-1]
-    cs = [pltpu.make_async_copy(refs[i], refs[n + i], sem.at[i]) for i in range(n)]
+    cs = []
+    for i in range(n):
+        rows = refs[i].shape[0] // CUTS[i]
+        for k in range(CUTS[i]):
+            at = pl.ds(k * rows, rows)
+            cs.append(pltpu.make_async_copy(refs[i].at[at], refs[n + i].at[at], sem.at[len(cs)]))
     for c in cs:
         c.start()
     for c in cs:
         c.wait()
+
+
+CUTS = (4, 1, 1, 4)
 
 
 def body(scale, tokens, blocks, left_factor, right_factor, upstream):
@@ -447,9 +455,9 @@
         V((rank, fb), BF), V((rows, fb), BF), V((rows, fb), F32), V((rows, fb), BF),
         V((rows, rank), F32), V((rows, rank), BF), V((7, part, rank), BF), V((rows, rank), BF), V((rank, rows), BF),
         V((rows, rank), F32), V((rows, rank), BF), V((7, part, rank), BF), V((rows, rank), BF),
-        V((3, rows, db), BF), V((3, rows, db), BF), V((rows, db), F32),
+        V((2, rows // NH, db // NK), BF), V((3, rows, db), BF), V((3, rows, db), BF), V((rows, db), F32),
         V((NC, rank, cw), BF), V((NC, rank // 2, cw), BF), V((NC, rank // 2, cw), BF),
-        V((NC, 3, rank // 8, cw), BF), V((NC, rank // 8, cw), BF), V((NC, rank // 4, cw), BF), V((2, rank // 4, cw), BF),
+        *[V((NC, 2, rank // 16, cw), BF)] * 4, V((NC, rank // 8, cw), BF), V((NC, rank // 8, cw), BF),
         V((db, rank), BF), V((db // 2, rank), BF), V((db // 2, rank), BF), V((7, db // 16, rank), BF),
         pltpu.SemaphoreType.DMA((8,)), pltpu.SemaphoreType.DMA((N_SEND,)), pltpu.SemaphoreType.DMA((N_RECV,)),
     ]
@@ -470,7 +478,7 @@
         out_shape=shapes,
         in_specs=[vmem_spec] * 4,
         out_specs=[any_spec] * 4,
-        scratch_shapes=[pltpu.SemaphoreType.DMA((4,))],
+        scratch_shapes=[pltpu.SemaphoreType.DMA((sum(CUTS),))],
         compiler_params=pltpu.CompilerParams(vmem_limit_bytes=1024 * 1024),
     )(*[pltpu.with_memory_space_constraint(r, pltpu.VMEM) for r in res])
 

time: 65.1 us -> 58.2 us (0.89)
  Pallas kernels: 64.2 us -> 57.2 us
    pallas_call x1, Pallas kernels: 62.2 us -> 55.2 us  [body(): pl.pallas_call(functools.partial(kernel, scale, (rows, db, fb, rank)), ou...]
where the time goes in v3:
time: 58.2 us; the launch traced here: 58 us
  Pallas kernels  57.2 us (98%)
  between operations  0.8 us (1%)
    pallas_call x1, Pallas kernels, body(): pl.pallas_call(functools.partial(kernel, scale, (rows, db, fb, rank)), ou...  55.2 us
    pallas_call x1, Pallas kernels, body(): pl.pallas_call(move, out_shape=shapes, in_specs=[vmem_spec] * 4, out_spec...  2 us

profile of v3, /device:TPU:1, one launch (start us, length us, event | category | flops | bytes accessed | tf_op | source)
XLA Modules:
  0.0 58.0 jit_solution(7035472166950160598)
XLA Ops:
  0.6 55.2 %shard_map.84 = (bf16[256,3072]{1,0:T(8,128)(2,1)S(1)}, bf16[256,768]{1,0:T(8,128)(2,1)S(1)}, bf16[768,256]{1,0:T(8,128)(2,1)S(1)}, bf16[256,3072]{1,0:T(8,128)(2,1)S(1)}) custom-call(bf16[256,768]{1,0:T(8,128)(2,1)} %tok_h.1, bf16[4,768,3072]{2,1,0:T(8,128)(2,1)} %blk_h.1, bf16[768,256]{1,0:T(8,128)(2,1)} %lf_h.1, bf16[256,3072]{1,0:T(8,128)(2,1)} %rf_h.1, ...), custom_call_target="tpu_custom_call" | custom-call | tf_op jit(solution)/shard_map/pallas_call | solution.py:466
  55.9 2.0 %shard_map.85 = (bf16[256,3072]{1,0:T(8,128)(2,1)}, bf16[256,768]{1,0:T(8,128)(2,1)}, bf16[768,256]{1,0:T(8,128)(2,1)}, bf16[256,3072]{1,0:T(8,128)(2,1)}) custom-call(bf16[256,3072]{1,0:T(8,128)(2,1)S(1)} %get-tuple-element.8.refs_0_, bf16[256,768]{1,0:T(8,128)(2,1)S(1)} %get-tuple-element.9.refs_1_, bf16[768,256]{1,0:T(8,128)(2,1)S(1)} %get-tuple-element.10.refs_2_, ...), custom_call_target="tpu_custom_call" | custom-call | tf_op jit(solution)/shard_map/pallas_call | solution.py:476

commit v4 on v3

--- a/solution.py
+++ b/solution.py
@@ -88,30 +88,32 @@
     l_rf = load(rf_h, rf)
     l_up = load(up_h, up)
 
-    groups = []
+    groups, slots = [], {}
 
     class Group:
-        def __init__(self, copies, size):
+        def __init__(self, copies, size, key=None):
             n = len(groups)
             if n >= N_SEND:
                 groups[n - N_SEND].sent()
-            self.ssem, self.rsem, self.size, self.open = send_sem.at[n % N_SEND], recv_sem.at[n], size, True
+            m = slots.setdefault(n if key is None else key, len(slots))
+            self.ssem, self.rsem, self.size, self.open = send_sem.at[n % N_SEND], recv_sem.at[m], size, True
             groups.append(self)
             for src, dst, to in copies:
                 pltpu.make_async_remote_copy(
                     src_ref=src, dst_ref=dst, send_sem=self.ssem, recv_sem=self.rsem,
                     device_id=to, device_id_type=MESH).start()
 
-        def got(self):
-            pltpu.make_async_copy(self.size, self.size, self.rsem).wait()
+        def got(self, size=None):
+            size = self.size if size is None else size
+            pltpu.make_async_copy(size, size, self.rsem).wait()
 
         def sent(self):
             if self.open:
                 pltpu.make_async_copy(self.size, self.size, self.ssem).wait()
                 self.open = False
 
-    def send(src, dst, to):
-        return Group([(src, dst, to)], dst)
+    def send(src, dst, to, key=None):
+        return Group([(src, dst, to)], dst, key)
 
     def scatter(src, dst):
         return Group([(src.at[pl.ds(flip(t, m) * part, part)], dst.at[m - 1], peer(m)) for m in (7, 5, 6, 4, 3, 1, 2)], dst)
@@ -161,12 +163,12 @@
     def relay_b(j):
         k, h = quads[NB + j]
         c_b[j].got()
-        c_z2b.append(send(rb.at[j], piece(3, k, h), peer(2)))
+        c_z2b.append(send(rb.at[j], piece(3, k, h), peer(2), "z2_%d" % k))
 
     def relay(i):
         k, h = quads[i]
         c_z1[i].got()
-        c_z2.append(send(piece(2, k, h), piece(3, k, h), peer(6)))
+        c_z2.append(send(piece(2, k, h), piece(3, k, h), peer(6), "z2_%d" % k))
 
     def own_fwd():
         l_blk[0].wait()
@@ -218,15 +220,14 @@
         c_xh[k].got()
 
     def w_z2(k):
-        for i in range(NH * k, NH * k + NH):
-            (c_z2[i] if i < NB else c_z2b[i - NB]).got()
+        c_z2[NH * k].got(tok.at[3, :, pl.ds(k * kw, kw)])
 
     def gelu(c):
         if c == 0:
             l_up.wait()
         cs = pl.ds(c * gw, gw)
         last = pl.ds((NK - 1) * kw, kw)
-        v = pre[:, cs] + mm(tok[3, :, last], blk[3, last, cs]) + mm(low[...], rf[:, cs])
+        v = pre[:, cs] + mm(jnp.concatenate([tok[3, :, last], low[...]], 1), jnp.concatenate([blk[3, last, cs], rf[:, cs]], 0))
         u = up[:, cs].astype(F32)
         v2 = v * v
         th = jnp.tanh(v * (C0 + (C0 * C1) * v2))
@@ -271,17 +272,16 @@
         g["p", c].got()
         rps[c] = (rp[c, pl.ds(core * half, half)].astype(F32) + rpair[c].astype(F32)).astype(BF)
         g["yr", c] = Group([(rps.at[c, rq(c, 2, 0)], yrl.at[c, 0], up_y), (rps.at[c, rq(c, 2, 1)], yrl.at[c, 1], dn_y)], yrl.at[c])
-        g["yf", c] = Group([(rps.at[c, rq(c, 1, 1)], yfin.at[c, 1], up_y), (rps.at[c, rq(c, 3, 0)], yfin.at[c, 0], dn_y)], yfin.at[c])
+        g["yf", c] = Group([(rps.at[c, rq(c, 1, 1)], yfin.at[c, 1], up_y), (rps.at[c, rq(c, 3, 0)], yfin.at[c, 0], dn_y)], yfin.at[c], "y_%d" % c)
 
     def r_s2b(c):
         g["yr", c].got()
         ybs[c, 0] = (rps[c, rq(c, 1, 0)].astype(F32) + yrl[c, 0].astype(F32)).astype(BF)
         ybs[c, 1] = (rps[c, rq(c, 3, 1)].astype(F32) + yrl[c, 1].astype(F32)).astype(BF)
-        g["yb", c] = Group([(ybs.at[c, 0], yb.at[c, 0], up_y), (ybs.at[c, 1], yb.at[c, 1], dn_y)], yb.at[c])
+        g["yb", c] = Group([(ybs.at[c, 0], yb.at[c, 0], up_y), (ybs.at[c, 1], yb.at[c, 1], dn_y)], yb.at[c], "y_%d" % c)
 
     def r_s3(c):
-        g["yf", c].got()
-        g["yb", c].got()
+        g["yf", c].got(rps.at[c, pl.ds(0, 4 * e)])
         for h in range(2):
             total = rps[c, rq(c, 0, h)].astype(F32) + yfin[c, h].astype(F32) + yb[c, h].astype(F32)
             rys[c, pl.ds(h * e, e)] = total.astype(BF)
@@ -303,10 +303,10 @@
     def r_a3(c):
         g["a2b", c].got()
         here = rgc(c, core * half, half)
-        g["a3", c] = send(here, here, pair)
-
-    def r_end(c):
-        g["a3", c].got()
+        g["a3", c] = send(here, here, pair, "a3")
+
+    def r_end():
+        g["a3", 0].got(rg.at[pl.ds(0, half)])
 
     def gcol(ref, i, k, n=NK):
         w = db // n
@@ -315,32 +315,31 @@
     NX = 6
 
     def p2(k):
-        ks = pl.ds(k * kw, kw)
+        ks = pl.ds(k * (db // 2), db // 2)
         gs[0, :, ks] = mm_t(slo[...], blk[3, ks, :]).astype(BF)
 
     def p2_send(k):
-        g["g2", k] = send(gcol(gs, 0, k, NX), gcol(gr, 0, k, NX), peer(6))
+        g["g2", k] = send(gcol(gs, 0, k, NX), gcol(gr, 0, k, NX), peer(6), "g2_%d" % (k // 2))
 
     def px(k):
-        ks = pl.ds(k * kw, kw)
+        ks = pl.ds(k * (db // 2), db // 2)
         gs[1, :, ks] = mm_t(slo[...], blk[1, ks, :]).astype(BF)
 
     def px_send(k):
-        g["gx", k] = send(gcol(gs, 1, k, NX), gcol(gr, 1, k, NX), peer(1))
+        g["gx", k] = send(gcol(gs, 1, k, NX), gcol(gr, 1, k, NX), peer(1), "gx")
 
     def p1(k):
-        ks = pl.ds(k * kw, kw)
+        ks = pl.ds(k * (db // 2), db // 2)
         pre[:, ks] = mm_t(slo[...], blk[2, ks, :])
 
     def p1_send(k):
         ks = pl.ds(k * kw, kw)
-        g["g2", 2 * k].got()
-        g["g2", 2 * k + 1].got()
+        g["g2", 2 * k].got(gcol(gr, 0, k))
         gs[2, :, ks] = (pre[:, ks] + gr[0, :, ks].astype(F32)).astype(BF)
-        g["g1", k] = send(gcol(gs, 2, k), gcol(gr, 2, k), peer(2))
+        g["g1", k] = send(gcol(gs, 2, k), gcol(gr, 2, k), peer(2), "g1")
 
     def p0(k):
-        ks = pl.ds(k * kw, kw)
+        ks = pl.ds(k * (db // 2), db // 2)
         own[:, ks] = mm_t(slo[...], blk[0, ks, :])
 
     lh, le = db // 2, db // 16
@@ -381,10 +380,8 @@
         g["lap"].got()
 
     def tg_end():
-        for k in range(NX):
-            g["gx", k].got()
-        for k in range(NK):
-            g["g1", k].got()
+        g["gx", 0].got(gr.at[1])
+        g["g1", 0].got(gr.at[2])
         tg[...] = (own[...] + gr[1].astype(F32) + gr[2].astype(F32)).astype(BF)
 
     def finish():
@@ -394,29 +391,29 @@
     OPS = dict(locals())
     for name, *a in ORDER:
         run(name, *a)
+    assert len(slots) == N_RECV
 
 
 ORDER = [
     ("start",), ("barrier",), ("send_z", 0), ("send_b", 0), ("low_rs_send",), ("send_z", 1), ("send_x", 0), ("send_b", 1),
     *[("send_z", i) for i in range(2, 8)], ("send_x", 1), *[("send_z", i) for i in range(8, 12)], ("send_x", 2), ("own_fwd",),
-    ("relay", 0), ("relay_b", 0), ("relay", 1), ("relay", 2), ("relay_b", 1), ("low_ag_send",), ("relay", 3), ("w_blk", 1), ("w_blk", 2),
+    ("relay", 0), ("relay_b", 0), ("relay", 1), ("low_ag_send",), ("relay", 2), ("relay_b", 1), ("relay", 3), ("w_blk", 1), ("w_blk", 2),
     ("add_k", 2, 0), ("relay", 4), ("relay", 5), ("w_xh", 0), ("add_k", 1, 0), ("relay", 6), ("relay", 7),
     ("add_k", 2, 1), ("relay", 8), ("relay", 9), ("w_xh", 1), ("add_k", 1, 1), ("w_z1", 10), ("w_z1", 11),
     ("add_k", 2, 2), ("w_blk", 3), ("w_z2", 0), ("add_k", 3, 0), ("w_xh", 2), ("add_k", 1, 2),
     ("w_z2", 1), ("add_k", 3, 1), ("w_low",), ("low_fwd",), ("w_z2", 2),
     ("gelu", 0), ("gelu", 1), ("r_s2", 0), ("r_s2", 1), ("gelu", 2), ("mix_send",), ("r_s2", 2), ("r_s2", 3),
     ("px", 0), ("px_send", 0), ("px_send", 1), ("r_s2", 4), ("r_s2", 5), ("r_s2b", 0), ("r_s2b", 1), ("px", 1), ("r_s2b", 2), ("r_s2b", 3),
-    ("px", 2), ("mix_ag_send",), ("r_s2b", 4), ("r_s2b", 5), ("r_s3", 0), ("r_s3", 1), ("px_send", 2), ("p2", 0), ("p2_send", 0), ("p2_send", 1),
-    ("r_s3", 2), ("r_s3", 3), ("p2", 1), ("p2_send", 2), ("p2_send", 3), ("r_s3", 4), ("r_s3", 5), ("r_a2", 0), ("left",), ("r_a2", 1), ("p2", 2), ("p2_send", 4), ("p2_send", 5),
-    ("px_send", 3), ("left_rs",), ("r_a2", 2), ("r_a2", 3), ("r_a2b", 0), ("p1", 0), ("p1_send", 0), ("px_send", 4), ("r_a2", 4), ("r_a2b", 1), ("r_a2", 5),
-    ("p1", 1), ("p1_send", 1), ("px_send", 5), ("p1", 2), ("p1_send", 2), ("r_a2b", 2), ("p0", 0), ("r_a2b", 3), ("r_a3", 0), ("left_ag",), ("p0", 1), ("r_a2b", 4), ("r_a3", 1), ("r_a2b", 5), ("p0", 2), ("r_a3", 2),
-    ("r_a3", 3), ("tg_low",), ("r_a3", 4), ("left_pair",), ("r_a3", 5), ("tg_end",),
-    *[("r_end", i) for i in range(6)], ("left_end",), ("finish",),
+    ("p2", 0), ("mix_ag_send",), ("p2_send", 0), ("p2_send", 1), ("r_s2b", 4), ("r_s2b", 5), ("r_s3", 0), ("r_s3", 1), ("px_send", 2), ("p2", 1), ("p2_send", 2),
+    ("r_s3", 2), ("r_s3", 3), ("p2_send", 3), ("r_s3", 4), ("r_s3", 5), ("p1", 0), ("r_a2", 0), ("p2_send", 4), ("left",), ("p2_send", 5), ("r_a2", 1),
+    ("px_send", 3), ("p1", 1), ("left_rs",), ("r_a2", 2), ("r_a2", 3), ("r_a2b", 0), ("p1_send", 0), ("px_send", 4), ("r_a2", 4), ("r_a2b", 1), ("r_a2", 5), ("p1_send", 1),
+    ("px_send", 5), ("p0", 0), ("p1_send", 2), ("r_a2b", 2), ("p0", 1), ("r_a2b", 3), ("r_a3", 0), ("left_ag",), ("tg_low",), ("r_a2b", 4), ("r_a3", 1), ("r_a2b", 5), ("r_a3", 2),
+    ("r_a3", 3), ("r_a3", 4), ("left_pair",), ("r_a3", 5), ("tg_end",), ("r_end",), ("left_end",), ("finish",),
 ]
 NB = 10
 NH = 4
 N_SEND = 20
-N_RECV = 100
+N_RECV = 70
 
 
 def move(*refs):

time: 58.2 us -> 57.5 us (0.988)
  Pallas kernels: 57.2 us -> 56.6 us
    pallas_call x1, Pallas kernels: 55.2 us -> 54.6 us  [body(): pl.pallas_call(functools.partial(kernel, scale, (rows, db, fb, rank)), ou...]
where the time goes in v4:
time: 57.5 us; the launch traced here: 57.4 us
  Pallas kernels  56.6 us (98%)
  between operations  0.8 us (1%)
    pallas_call x1, Pallas kernels, body(): pl.pallas_call(functools.partial(kernel, scale, (rows, db, fb, rank)), ou...  54.6 us
    pallas_call x1, Pallas kernels, body(): pl.pallas_call(move, out_shape=shapes, in_specs=[vmem_spec] * 4, out_spec...  2 us

profile of v4, /device:TPU:1, one launch (start us, length us, event | category | flops | bytes accessed | tf_op | source)
XLA Modules:
  0.0 57.4 jit_solution(11987797772868220526)
XLA Ops:
  0.6 54.6 %shard_map.84 = (bf16[256,3072]{1,0:T(8,128)(2,1)S(1)}, bf16[256,768]{1,0:T(8,128)(2,1)S(1)}, bf16[768,256]{1,0:T(8,128)(2,1)S(1)}, bf16[256,3072]{1,0:T(8,128)(2,1)S(1)}) custom-call(bf16[256,768]{1,0:T(8,128)(2,1)} %tok_h.1, bf16[4,768,3072]{2,1,0:T(8,128)(2,1)} %blk_h.1, bf16[768,256]{1,0:T(8,128)(2,1)} %lf_h.1, bf16[256,3072]{1,0:T(8,128)(2,1)} %rf_h.1, ...), custom_call_target="tpu_custom_call" | custom-call | tf_op jit(solution)/shard_map/pallas_call | solution.py:463
  55.3 2.0 %shard_map.85 = (bf16[256,3072]{1,0:T(8,128)(2,1)}, bf16[256,768]{1,0:T(8,128)(2,1)}, bf16[768,256]{1,0:T(8,128)(2,1)}, bf16[256,3072]{1,0:T(8,128)(2,1)}) custom-call(bf16[256,3072]{1,0:T(8,128)(2,1)S(1)} %get-tuple-element.8.refs_0_, bf16[256,768]{1,0:T(8,128)(2,1)S(1)} %get-tuple-element.9.refs_1_, bf16[768,256]{1,0:T(8,128)(2,1)S(1)} %get-tuple-element.10.refs_2_, ...), custom_call_target="tpu_custom_call" | custom-call | tf_op jit(solution)/shard_map/pallas_call | solution.py:473

commit v5 on v4

--- a/solution.py
+++ b/solution.py
@@ -404,9 +404,9 @@
     ("w_z2", 1), ("add_k", 3, 1), ("w_low",), ("low_fwd",), ("w_z2", 2),
     ("gelu", 0), ("gelu", 1), ("r_s2", 0), ("r_s2", 1), ("gelu", 2), ("mix_send",), ("r_s2", 2), ("r_s2", 3),
     ("px", 0), ("px_send", 0), ("px_send", 1), ("r_s2", 4), ("r_s2", 5), ("r_s2b", 0), ("r_s2b", 1), ("px", 1), ("r_s2b", 2), ("r_s2b", 3),
-    ("p2", 0), ("mix_ag_send",), ("p2_send", 0), ("p2_send", 1), ("r_s2b", 4), ("r_s2b", 5), ("r_s3", 0), ("r_s3", 1), ("px_send", 2), ("p2", 1), ("p2_send", 2),
-    ("r_s3", 2), ("r_s3", 3), ("p2_send", 3), ("r_s3", 4), ("r_s3", 5), ("p1", 0), ("r_a2", 0), ("p2_send", 4), ("left",), ("p2_send", 5), ("r_a2", 1),
-    ("px_send", 3), ("p1", 1), ("left_rs",), ("r_a2", 2), ("r_a2", 3), ("r_a2b", 0), ("p1_send", 0), ("px_send", 4), ("r_a2", 4), ("r_a2b", 1), ("r_a2", 5), ("p1_send", 1),
+    ("p2", 0), ("mix_ag_send",), ("p2_send", 0), ("p2_send", 1), ("r_s2b", 4), ("r_s2b", 5), ("r_s3", 0), ("r_s3", 1), ("p2", 1), ("p2_send", 2),
+    ("r_s3", 2), ("r_s3", 3), ("px_send", 2), ("p2_send", 3), ("r_s3", 4), ("r_s3", 5), ("px_send", 3), ("r_a2", 0), ("p2_send", 4), ("left",), ("p2_send", 5), ("r_a2", 1), ("r_a2", 2), ("p1", 0),
+    ("r_a2", 3), ("left_rs",), ("p1", 1), ("r_a2b", 0), ("p1_send", 0), ("px_send", 4), ("r_a2", 4), ("r_a2b", 1), ("r_a2", 5), ("p1_send", 1),
     ("px_send", 5), ("p0", 0), ("p1_send", 2), ("r_a2b", 2), ("p0", 1), ("r_a2b", 3), ("r_a3", 0), ("left_ag",), ("tg_low",), ("r_a2b", 4), ("r_a3", 1), ("r_a2b", 5), ("r_a3", 2),
     ("r_a3", 3), ("r_a3", 4), ("left_pair",), ("r_a3", 5), ("tg_end",), ("r_end",), ("left_end",), ("finish",),
 ]
@@ -431,7 +431,7 @@
         c.wait()
 
 
-CUTS = (4, 1, 1, 4)
+CUTS = (1, 1, 1, 1)
 
 
 def body(scale, tokens, blocks, left_factor, right_factor, upstream):

time: 57.5 us -> 56.5 us (0.983)
  Pallas kernels: 56.6 us -> 55.6 us
    pallas_call x1, Pallas kernels: 54.6 us -> 53.6 us  [body(): pl.pallas_call(functools.partial(kernel, scale, (rows, db, fb, rank)), ou...]
where the time goes in v5:
time: 56.5 us; the launch traced here: 56.4 us
  Pallas kernels  55.6 us (98%)
  between operations  0.8 us (1%)
    pallas_call x1, Pallas kernels, body(): pl.pallas_call(functools.partial(kernel, scale, (rows, db, fb, rank)), ou...  53.6 us
    pallas_call x1, Pallas kernels, body(): pl.pallas_call(move, out_shape=shapes, in_specs=[vmem_spec] * 4, out_spec...  1.96 us

profile of v5, /device:TPU:1, one launch (start us, length us, event | category | flops | bytes accessed | tf_op | source)
XLA Modules:
  0.0 56.4 jit_solution(12889124826291214489)
XLA Ops:
  0.6 53.6 %shard_map.84 = (bf16[256,3072]{1,0:T(8,128)(2,1)S(1)}, bf16[256,768]{1,0:T(8,128)(2,1)S(1)}, bf16[768,256]{1,0:T(8,128)(2,1)S(1)}, bf16[256,3072]{1,0:T(8,128)(2,1)S(1)}) custom-call(bf16[256,768]{1,0:T(8,128)(2,1)} %tok_h.1, bf16[4,768,3072]{2,1,0:T(8,128)(2,1)} %blk_h.1, bf16[768,256]{1,0:T(8,128)(2,1)} %lf_h.1, bf16[256,3072]{1,0:T(8,128)(2,1)} %rf_h.1, ...), custom_call_target="tpu_custom_call" | custom-call | tf_op jit(solution)/shard_map/pallas_call | solution.py:463
  54.2 2.0 %shard_map.85 = (bf16[256,3072]{1,0:T(8,128)(2,1)}, bf16[256,768]{1,0:T(8,128)(2,1)}, bf16[768,256]{1,0:T(8,128)(2,1)}, bf16[256,3072]{1,0:T(8,128)(2,1)}) custom-call(bf16[256,3072]{1,0:T(8,128)(2,1)S(1)} %get-tuple-element.8.refs_0_, bf16[256,768]{1,0:T(8,128)(2,1)S(1)} %get-tuple-element.9.refs_1_, bf16[768,256]{1,0:T(8,128)(2,1)S(1)} %get-tuple-element.10.refs_2_, ...), custom_call_target="tpu_custom_call" | custom-call | tf_op jit(solution)/shard_map/pallas_call | solution.py:473

commit v6 on v5

--- a/solution.py
+++ b/solution.py
@@ -395,7 +395,7 @@
 
 
 ORDER = [
-    ("start",), ("barrier",), ("send_z", 0), ("send_b", 0), ("low_rs_send",), ("send_z", 1), ("send_x", 0), ("send_b", 1),
+    ("barrier",), ("send_z", 0), ("send_b", 0), ("start",), ("low_rs_send",), ("send_z", 1), ("send_x", 0), ("send_b", 1),
     *[("send_z", i) for i in range(2, 8)], ("send_x", 1), *[("send_z", i) for i in range(8, 12)], ("send_x", 2), ("own_fwd",),
     ("relay", 0), ("relay_b", 0), ("relay", 1), ("low_ag_send",), ("relay", 2), ("relay_b", 1), ("relay", 3), ("w_blk", 1), ("w_blk", 2),
     ("add_k", 2, 0), ("relay", 4), ("relay", 5), ("w_xh", 0), ("add_k", 1, 0), ("relay", 6), ("relay", 7),
@@ -405,7 +405,7 @@
     ("gelu", 0), ("gelu", 1), ("r_s2", 0), ("r_s2", 1), ("gelu", 2), ("mix_send",), ("r_s2", 2), ("r_s2", 3),
     ("px", 0), ("px_send", 0), ("px_send", 1), ("r_s2", 4), ("r_s2", 5), ("r_s2b", 0), ("r_s2b", 1), ("px", 1), ("r_s2b", 2), ("r_s2b", 3),
     ("p2", 0), ("mix_ag_send",), ("p2_send", 0), ("p2_send", 1), ("r_s2b", 4), ("r_s2b", 5), ("r_s3", 0), ("r_s3", 1), ("p2", 1), ("p2_send", 2),
-    ("r_s3", 2), ("r_s3", 3), ("px_send", 2), ("p2_send", 3), ("r_s3", 4), ("r_s3", 5), ("px_send", 3), ("r_a2", 0), ("p2_send", 4), ("left",), ("p2_send", 5), ("r_a2", 1), ("r_a2", 2), ("p1", 0),
+    ("r_s3", 2), ("r_s3", 3), ("px_send", 2), ("p2_send", 3), ("r_s3", 4), ("r_s3", 5), ("r_a2", 0), ("p2_send", 4), ("left",), ("p2_send", 5), ("r_a2", 1), ("r_a2", 2), ("px_send", 3), ("p1", 0),
     ("r_a2", 3), ("left_rs",), ("p1", 1), ("r_a2b", 0), ("p1_send", 0), ("px_send", 4), ("r_a2", 4), ("r_a2b", 1), ("r_a2", 5), ("p1_send", 1),
     ("px_send", 5), ("p0", 0), ("p1_send", 2), ("r_a2b", 2), ("p0", 1), ("r_a2b", 3), ("r_a3", 0), ("left_ag",), ("tg_low",), ("r_a2b", 4), ("r_a3", 1), ("r_a2b", 5), ("r_a3", 2),
     ("r_a3", 3), ("r_a3", 4), ("left_pair",), ("r_a3", 5), ("tg_end",), ("r_end",), ("left_end",), ("finish",),

time: 56.5 us -> 56.5 us (level)
  no operation moved by 1% of the time
where the time goes in v6:
time: 56.5 us; the launch traced here: 56.3 us
  Pallas kernels  55.5 us (98%)
  between operations  0.8 us (1%)
    pallas_call x1, Pallas kernels, body(): pl.pallas_call(functools.partial(kernel, scale, (rows, db, fb, rank)), ou...  53.6 us
    pallas_call x1, Pallas kernels, body(): pl.pallas_call(move, out_shape=shapes, in_specs=[vmem_spec] * 4, out_spec...  1.96 us

profile of v6, /device:TPU:1, one launch (start us, length us, event | category | flops | bytes accessed | tf_op | source)
XLA Modules:
  0.0 56.3 jit_solution(8267718155458826290)
XLA Ops:
  0.6 53.6 %shard_map.84 = (bf16[256,3072]{1,0:T(8,128)(2,1)S(1)}, bf16[256,768]{1,0:T(8,128)(2,1)S(1)}, bf16[768,256]{1,0:T(8,128)(2,1)S(1)}, bf16[256,3072]{1,0:T(8,128)(2,1)S(1)}) custom-call(bf16[256,768]{1,0:T(8,128)(2,1)} %tok_h.1, bf16[4,768,3072]{2,1,0:T(8,128)(2,1)} %blk_h.1, bf16[768,256]{1,0:T(8,128)(2,1)} %lf_h.1, bf16[256,3072]{1,0:T(8,128)(2,1)} %rf_h.1, ...), custom_call_target="tpu_custom_call" | custom-call | tf_op jit(solution)/shard_map/pallas_call | solution.py:463
  54.2 2.0 %shard_map.85 = (bf16[256,3072]{1,0:T(8,128)(2,1)}, bf16[256,768]{1,0:T(8,128)(2,1)}, bf16[768,256]{1,0:T(8,128)(2,1)}, bf16[256,3072]{1,0:T(8,128)(2,1)}) custom-call(bf16[256,3072]{1,0:T(8,128)(2,1)S(1)} %get-tuple-element.8.refs_0_, bf16[256,768]{1,0:T(8,128)(2,1)S(1)} %get-tuple-element.9.refs_1_, bf16[768,256]{1,0:T(8,128)(2,1)S(1)} %get-tuple-element.10.refs_2_, ...), custom_call_target="tpu_custom_call" | custom-call | tf_op jit(solution)/shard_map/pallas_call | solution.py:473
